TPU v7x, 32 devices: a whole 2x2x4 slice. The times are simulated.
32 devices in a mesh: groups: 2 (over x), rows: 16 (over z, y, core).
Axes of the slice: x: 2, y: 2, z: 4, core: 2. Of those that a mesh axis runs over, the one named last changes fastest.
Arguments:
- ensemble: float32 [131072, 256], P(('groups', 'rows')), parts along dimension 0, may hold values from -60 to 60
- mean_state: float32 [131072], P(('groups', 'rows')), parts along dimension 0, may hold values from -6 to 6
- observed: float32 [4, 128], P('groups'), parts along dimension 0, may hold values from -8 to 8
- error_var: float32 [4, 128], P('groups'), parts along dimension 0, may hold values from 0.5 to 4
- owner: int32 [4], P('groups'), parts along dimension 0, may hold values from 0 to 15
- obs_rows: int32 [4, 128], P('groups'), parts along dimension 0, may hold values from 0 to 4095
Outputs:
- analysis_ensemble: float32 [131072, 256], P(('groups', 'rows')), parts along dimension 0
- analysis_mean: float32 [131072], P(('groups', 'rows')), parts along dimension 0
There are 2 independent parts, one for each index of `groups`. A program takes and returns all parts, laid end to end along the dimension named above; each array names one. Nothing has to cross between parts.
Inputs may be any that keep to these rules, and one draw needn't show every extreme that they name: `obs_rows`: rows may repeat.
All inputs are finite; a program needn't handle non-finite values.
Results may differ from a plain program's by a relative error of at most 0.0003.
Values sent between devices are 32-bit elements; how exact they have to be, the bound alone decides.
No kernel may reach another device: no remote copies, remote signals or barrier semaphores. Data moves between devices by JAX's collectives and lax.ppermute only.
A program may use at most 64 MiB of HBM per device.

v0:
```python
import functools

import jax
import jax.numpy as jnp
from jax import lax
from jax.experimental import pallas as pl
from jax.experimental.pallas import tpu as pltpu
from jax.sharding import PartitionSpec as P

RELAX = 0.6
HI = lax.Precision.HIGHEST
AXIS = "rows"
F32 = jnp.float32
BF16 = jnp.bfloat16
LANES = 128
SUB = 8
OBS = 128
VMEM_LIMIT = 51 * 1024 * 1024
STEP = 16
SCALE = 2.0**-16

A0, A1, B0, B1, G00, G01, G11 = range(0, 7 * 128, 128)
PACKED = G11 + 64
INNOV = G00 + 96
INNOV_LANES = 32


def dot(a, b, dims=((1,), (0,)), precision=HI):
    return lax.dot_general(a, b, (dims, ((), ())), precision=precision, preferred_element_type=F32)


def column(row):
    return jnp.broadcast_to(row, (LANES, LANES)).T


def split(x):
    high = x.astype(BF16)
    return high, (x - high.astype(F32)).astype(BF16)


def chunk_copy(source, target, sem, chunks):
    size = source.shape[0] // chunks

    def copy(i):
        part = pl.ds(i * size, size)
        return pltpu.make_async_copy(source.at[part], target.at[part], sem.at[i])

    return copy


def gram_kernel(chunks, x_hbm, out, x_buf, sem):
    members = x_buf.shape[1]
    size = x_buf.shape[0] // chunks
    half = members // 2
    copy = chunk_copy(x_hbm, x_buf, sem, chunks)
    for i in range(chunks):
        copy(i).start()
    total = None
    for i in range(chunks):
        copy(i).wait()
        high, low = split(x_buf[i * size : (i + 1) * size, :])
        part = dot(high, jnp.concatenate([high, low], axis=1), ((0,), (0,)), None)
        total = part if total is None else total + part
    cross = total[:, members:]
    total = total[:, :members] + cross + cross.T
    quarter = half // 2
    out[:quarter, :] = total[:quarter, :half]
    out[quarter:half, :] = jnp.concatenate(
        [total[half + quarter :, half + quarter :], total[quarter:half, quarter:half]], axis=1
    )
    out[half : 2 * half, :] = total[:half, half:]
    out[2 * half :, :] = total[half : half + quarter, half:]


def gather_kernel(
    owner_s, rows_s, rows_v, observed, error_var, mean_v, gram, x_hbm, keep, send, full, picked, sem
):
    me = lax.axis_index(AXIS)
    members = picked.shape[2]
    half = members // 2

    full[:G00, :] = jnp.zeros((G00, LANES), F32)
    full[G00:, :] = gram[...]
    full[INNOV : INNOV + 2 * OBS // INNOV_LANES, :INNOV_LANES] = jnp.zeros((2 * OBS // INNOV_LANES, INNOV_LANES), F32)
    lane = lax.broadcasted_iota(jnp.int32, (OBS, LANES), 1)
    lines = mean_v.shape[0]
    fetches = OBS // lines

    for k, left, right in ((0, A0, A1), (1, B0, B1)):

        @pl.when(owner_s[k] == me)
        def _(k=k, left=left, right=right):
            index = column(rows_v[k : k + 1, :].astype(F32)).astype(jnp.int32) - lane

            def look(r, prior):
                for j in range(fetches):
                    o = r * fetches + j
                    pltpu.make_async_copy(
                        x_hbm.at[pl.ds(rows_s[k, o], 1)], picked.at[k, pl.ds(o, 1)], sem.at[k]
                    ).start()
                return prior + jnp.where(index == r * LANES, mean_v[pl.ds(r, 1), :], 0.0)

            prior = lax.fori_loop(0, lines, look, jnp.zeros((OBS, LANES), F32), unroll=8)
            prior = jnp.sum(prior.T, axis=0, keepdims=True)
            scale = lax.rsqrt(error_var[k : k + 1, :] * (members - 1.0))
            innov = scale * (observed[k : k + 1, :] - prior)
            count = OBS // INNOV_LANES
            for j in range(count):
                at = INNOV + count * k + j
                full[at : at + 1, :INNOV_LANES] = innov[:, j * INNOV_LANES : (j + 1) * INNOV_LANES]
            scales = column(scale)
            pltpu.make_async_copy(x_hbm.at[pl.ds(0, OBS)], picked.at[k], sem.at[k]).wait()
            full[left : left + OBS, :] = picked[k, :, :half] * scales
            full[right : right + OBS, :] = picked[k, :, half:] * scales

    mine = me & 1
    span = PACKED // 2
    keep[...] = full[pl.ds(pl.multiple_of(mine * span, SUB), span), :]
    send[...] = full[pl.ds(pl.multiple_of((1 - mine) * span, SUB), span), :]


def tree(terms):
    while len(terms) > 1:
        terms = [terms[i] + terms[i + 1] if i + 1 < len(terms) else terms[i] for i in range(0, len(terms), 2)]
    return terms[0]


def factor(a):
    a = a * SCALE
    count = LANES // SUB
    lane = lax.broadcasted_iota(jnp.int32, (SUB, LANES), 1)
    sub = lax.broadcasted_iota(jnp.int32, (SUB, LANES), 0)
    rows = [a[SUB * i : SUB * (i + 1), :] for i in range(count)]
    out = []

    def spread(x, c):
        return jnp.broadcast_to(x[:, c : c + 1], (SUB, LANES))

    def row(x, j):
        return jnp.broadcast_to(x[j : j + 1, :], (SUB, LANES))

    groups = STEP // SUB
    for s in range(0, count, groups):
        base = SUB * s
        here = (lane >= base) & (lane < base + STEP)
        cols = [[spread(rows[s + g], base + q) for g in range(groups)] for q in range(STEP)]
        work = [
            jnp.where(here, (lane - base == sub + SUB * g).astype(F32), rows[s + g]) for g in range(groups)
        ]
        done = [jnp.zeros((SUB, LANES), F32) for _ in range(groups)]
        for p in range(0, STEP, 2):
            at, j = divmod(p, SUB)
            first, second = sub == j, sub == j + 1
            pair = first | second
            pa, pb, pc = row(cols[p][at], j), row(cols[p][at], j + 1), row(cols[p + 1][at], j + 1)
            det = pa * pc - pb * pb
            if p % 4 == 0:
                inv = pl.reciprocal(det, approx=True)
                third, fourth = cols[p + 2][at], cols[p + 3][at]
                b00, b10, b01, b11 = row(third, j), row(third, j + 1), row(fourth, j), row(fourth, j + 1)
                w00, w10 = pc * b00 - pb * b10, pa * b10 - pb * b00
                w01, w11 = pc * b01 - pb * b11, pa * b11 - pb * b01
                s0 = det * row(third, j + 2) - (b00 * w00 + b10 * w10)
                s1 = det * row(third, j + 3) - (b00 * w01 + b10 * w11)
                s2 = det * row(fourth, j + 3) - (b01 * w01 + b11 * w11)
                next_inv = (det * det) * pl.reciprocal(s0 * s2 - s1 * s1, approx=True)
            else:
                inv = next_inv
            top, low = row(work[at], j), row(work[at], j + 1)
            done[at] = jnp.where(first, top * lax.rsqrt(pa), done[at])
            done[at] = jnp.where(second, (pa * low - pb * top) * lax.rsqrt(pa * det), done[at])
            raw, scaled = [], []
            for g in range(groups):
                m0, m1 = cols[p][g], cols[p + 1][g]
                if g == at:
                    m0 = jnp.where(first, -1.0, jnp.where(second, 0.0, m0))
                    m1 = jnp.where(second, -1.0, jnp.where(first, 0.0, m1))
                u0, u1 = m0 * pc - m1 * pb, m1 * pa - m0 * pb
                raw.append((u0, u1))
                scaled.append((u0 * inv, u1 * inv))
            for q in range(p + 2, STEP + 1):
                kept = cols[q] if q < STEP else work
                t, l = row(kept[at], j), row(kept[at], j + 1)
                moved = []
                for g in range(groups):
                    old = jnp.where(pair, 0.0, kept[g]) if g == at else kept[g]
                    if q < p + 4:
                        moved.append(old - (raw[g][0] * t + raw[g][1] * l) * inv)
                    else:
                        moved.append(old - (scaled[g][0] * t + scaled[g][1] * l))
                if q < STEP:
                    cols[q] = moved
                else:
                    work = moved
        for g in range(groups):
            out.append(jnp.where(lane <= base + SUB * g + sub, done[g], 0.0))
        lines = [row(work[p // SUB], p % SUB) for p in range(STEP)]
        later = s + 2 * groups
        for i in range(s + groups, min(later, count)):
            change = tree([spread(rows[i], base + p) * lines[p] for p in range(STEP)])
            rows[i] = jnp.where(here, 0.0, rows[i]) - change
        if later < count:
            rest = jnp.concatenate(rows[later:], axis=0)
            inside = jnp.concatenate([here] * (count - later), axis=0)
            pieces = [jnp.zeros((base, LANES), F32)] if base else []
            pieces += work + [jnp.zeros((LANES - base - STEP, LANES), F32)]
            change = dot(jnp.where(inside, rest, 0.0), jnp.concatenate(pieces, axis=0))
            rest = jnp.where(inside, 0.0, rest) - change
            rows[later:] = [rest[SUB * i : SUB * (i + 1), :] for i in range(count - later)]
    return jnp.concatenate(out, axis=0) * SCALE**0.5


def blend(before, after):
    return 1.0 + RELAX * (jnp.sqrt(before / after) - 1.0)


def add_up(x):
    return jnp.sum(jnp.sum(x, axis=0, keepdims=True), axis=1, keepdims=True)


def dot3(a, b):
    a_high, a_low = split(a)
    b_high, b_low = split(b)
    left = jnp.concatenate([a_high, a_low, a_high], axis=1)
    return dot(left, jnp.concatenate([b_high, b_high, b_low], axis=0), precision=None)


def identity(size):
    return (
        lax.broadcasted_iota(jnp.int32, (size, size), 0) == lax.broadcasted_iota(jnp.int32, (size, size), 1)
    ).astype(F32)


def update_kernel(
    chunks, mine_v, other_v, mean_v, x_hbm, out_hbm, mean_out, full, x_buf, o_buf, in_sem, out_sem
):
    members = x_buf.shape[1]
    size = x_buf.shape[0] // chunks
    load = chunk_copy(x_hbm, x_buf, in_sem, chunks)
    store = chunk_copy(o_buf, out_hbm, out_sem, chunks)
    for i in range(chunks):
        load(i).start()

    mine = lax.axis_index(AXIS) & 1
    span = PACKED // 2
    full[pl.ds(pl.multiple_of(mine * span, SUB), span), :] = mine_v[...]
    full[pl.ds(pl.multiple_of((1 - mine) * span, SUB), span), :] = other_v[...]

    half = members // 2
    quarter = half // 2

    def block(at):
        return full[at : at + half, :]

    def innovation(k):
        count = OBS // INNOV_LANES
        at = INNOV + count * k
        return column(jnp.concatenate([full[at + j : at + j + 1, :INNOV_LANES] for j in range(count)], axis=1))

    first = jnp.concatenate([block(A0), block(A1)], axis=1)
    second = jnp.concatenate([block(B0), block(B1)], axis=1)
    g00, g01, top = block(G00), block(G01), full[G11:, :]
    line = lax.broadcasted_iota(jnp.int32, (half, half), 0)
    lane = lax.broadcasted_iota(jnp.int32, (half, half), 1)
    last = jnp.concatenate([jnp.zeros((quarter, quarter), F32), g00[quarter:, :quarter]], axis=1)
    corner = (line >= quarter) & (lane < quarter)
    g00 = jnp.where(corner, g00.T, g00)
    g11 = jnp.concatenate([top, last], axis=0)
    inner = (line >= INNOV - G00) & (lane >= quarter) & (lane < quarter + INNOV_LANES)
    g11 = jnp.where(corner | inner, g11.T, g11)
    gram = jnp.concatenate(
        [jnp.concatenate([g00, g01], axis=1), jnp.concatenate([g01.T, g11], axis=1)], axis=0
    )
    eye = identity(half)

    inv_m = factor(eye + dot(first, first, ((1,), (1,))))
    v_and_f = dot(inv_m, jnp.concatenate([first, innovation(0)], axis=1))
    v, f = v_and_f[:, :members], v_and_f[:, members:]
    before = add_up(eye * (g00 + g11))
    after1 = before - add_up(dot3(v, gram) * v)
    factor1 = blend(before, after1)
    increment = jnp.sum(v * jnp.concatenate([f, f], axis=1), axis=0, keepdims=True)
    innov2 = innovation(1) - jnp.sum(second * increment, axis=1, keepdims=True)

    a1 = dot(first, first, ((0,), (0,)))
    a2 = dot(second, second, ((0,), (0,)))
    square = factor1 * factor1
    k00 = eye + a1[:half, :half] + a2[:half, :half] * square
    k01 = a1[:half, half:] + a2[:half, half:] * square
    k11 = eye + a1[half:, half:] + a2[half:, half:] * square
    inv00 = factor(k00)
    u = dot(inv00, k01)
    inv11 = factor(k11 - dot(u, u, ((0,), (0,))))
    inv10 = -dot(inv11, dot(u, inv00, ((0,), (0,))))
    target = dot(second, innov2, ((0,), (0,))) * square
    y0 = dot(inv00, target[:half, :])
    y1 = dot(inv11, target[half:, :] - dot(u, y0, ((0,), (0,))))
    bottom = jnp.concatenate([inv10, inv11], axis=1)
    top_trace = add_up(dot3(inv00, g00) * inv00)
    after2 = top_trace + add_up(dot3(bottom, gram) * bottom)
    factor2 = factor1 * blend(after1, after2)
    increment0 = jnp.sum(y0 * inv00 + y1 * inv10, axis=0, keepdims=True)
    increment1 = jnp.sum(y1 * inv11, axis=0, keepdims=True)
    increment = increment + jnp.concatenate([increment0, increment1], axis=1)

    turned = jnp.concatenate(
        [jnp.concatenate([inv00.T, inv10.T], axis=1), jnp.concatenate([jnp.zeros_like(inv00), inv11.T], axis=1)], axis=0
    )
    high, low = split(turned)
    transform = jnp.concatenate([high, high, low], axis=0)
    step_line = lax.broadcasted_iota(jnp.int32, (LANES, LANES), 0)
    diagonal = step_line == lax.broadcasted_iota(jnp.int32, (LANES, LANES), 1)

    def apply(i, at):
        load(i).wait()
        x = x_buf[pl.ds(at, size), :]
        high, low = split(x)
        moved = dot(jnp.concatenate([high, low, high], axis=1), transform, precision=None)
        o_buf[pl.ds(at, size), :] = moved * factor2
        store(i).start()
        steps = jnp.sum(x * increment, axis=1, keepdims=True)
        for j in range(0, size, LANES):
            step = jnp.sum(jnp.where(diagonal, steps[j : j + LANES, :], 0.0), axis=0, keepdims=True)
            part = pl.ds(at + j, LANES)
            mean_out[:, part] = mean_v[:, part] + step

    apply(0, 0)

    def body(i, _):
        apply(i, pl.multiple_of(i * size, size))
        return 0

    lax.fori_loop(1, chunks, body, 0)
    for i in range(chunks):
        store(i).wait()


def spec(space):
    return pl.BlockSpec(memory_space=space)


def params():
    return pltpu.CompilerParams(vmem_limit_bytes=VMEM_LIMIT)


def cost(flops, bytes_accessed):
    return pl.CostEstimate(flops=flops, bytes_accessed=bytes_accessed, transcendentals=0)


def cost(flops, bytes_accessed):
    return pl.CostEstimate(flops=flops, bytes_accessed=bytes_accessed, transcendentals=0)


def gram_of(ensemble):
    rows, members = ensemble.shape
    chunks = 4
    return pl.pallas_call(
        functools.partial(gram_kernel, chunks),
        out_shape=jax.ShapeDtypeStruct((PACKED - G00, LANES), F32),
        in_specs=[spec(pltpu.HBM)],
        out_specs=spec(pltpu.VMEM),
        scratch_shapes=[pltpu.VMEM((rows, members), F32), pltpu.SemaphoreType.DMA((chunks,))],
        cost_estimate=cost(4 * rows * members * members, 4 * rows * members),
        compiler_params=params(),
    )(ensemble)


def gather(ensemble, mean_state, observed, error_var, owner, obs_rows, gram):
    members = ensemble.shape[1]
    half = jax.ShapeDtypeStruct((PACKED // 2, LANES), F32)
    return pl.pallas_call(
        gather_kernel,
        out_shape=(half, half),
        in_specs=[spec(pltpu.SMEM), spec(pltpu.SMEM)] + [spec(pltpu.VMEM)] * 5 + [spec(pltpu.HBM)],
        out_specs=[spec(pltpu.VMEM)] * 2,
        scratch_shapes=[
            pltpu.VMEM((PACKED, LANES), F32),
            pltpu.VMEM((2, OBS, members), F32),
            pltpu.SemaphoreType.DMA((2,)),
        ],
        compiler_params=params(),
    )(owner, obs_rows, obs_rows, observed, error_var, mean_state.reshape(-1, LANES), gram, ensemble)


def update(packed, ensemble, mean_state):
    rows, members = ensemble.shape
    chunks = 4
    out, mean = pl.pallas_call(
        functools.partial(update_kernel, chunks),
        out_shape=(jax.ShapeDtypeStruct((rows, members), F32), jax.ShapeDtypeStruct((1, rows), F32)),
        in_specs=[spec(pltpu.VMEM)] * 3 + [spec(pltpu.HBM)],
        out_specs=(spec(pltpu.HBM), spec(pltpu.VMEM)),
        scratch_shapes=[
            pltpu.VMEM((PACKED, LANES), F32),
            pltpu.VMEM((rows, members), F32),
            pltpu.VMEM((rows, members), F32),
            pltpu.SemaphoreType.DMA((chunks,)),
            pltpu.SemaphoreType.DMA((chunks,)),
        ],
        compiler_params=params(),
    )(*packed, mean_state.reshape(1, rows), ensemble)
    return out, mean.reshape(rows)


def swap(value, count, mask):
    return lax.ppermute(value, AXIS, [(i, i ^ mask) for i in range(count)])


def total(keep, send, count):
    odd = ((lax.axis_index(AXIS) >> 1) & 1) == 1
    value = keep + swap(send, count, 1)
    low, high = jnp.split(value, 2, axis=0)
    value = jnp.where(odd, high, low) + swap(jnp.where(odd, low, high), count, 2)
    mask = 4
    while mask < count:
        value = value + swap(value, count, mask)
        mask *= 2
    got = swap(value, count, 2)
    value = jnp.concatenate([jnp.where(odd, got, value), jnp.where(odd, value, got)], axis=0)
    return value, swap(value, count, 1)


def on_device(count, ensemble, mean_state, observed, error_var, owner, obs_rows):
    gram = gram_of(ensemble)
    keep, send = gather(ensemble, mean_state, observed, error_var, owner, obs_rows, gram)
    return update(total(keep, send, count), ensemble, mean_state)


def solution(mesh):
    count = mesh.shape[AXIS]
    in_specs = (
        P(("groups", "rows"), None),
        P(("groups", "rows")),
        P("groups", None),
        P("groups", None),
        P("groups"),
        P("groups", None),
    )
    out_specs = (P(("groups", "rows"), None), P(("groups", "rows")))

    def body(*args):
        return on_device(count, *args)

    return jax.shard_map(body, mesh=mesh, in_specs=in_specs, out_specs=out_specs, check_vma=False)
```

profile of v0, /device:TPU:0, one launch (start us, length us, event | category | flops | bytes accessed | tf_op | source)
XLA Modules:
  0.0 46.7 jit_solution(18046459992499837049)
XLA Ops:
  0.6 0.0 copy-start
  0.6 0.0 copy-start.1
  0.7 0.0 copy-start.4
  0.7 0.0 copy-start.3
  0.7 0.0 copy-start.2
  0.7 3.4 %shard_map.77.gram = f32[320,128]{1,0:T(8,128)S(1)} custom-call(f32[4096,256]{1,0:T(8,128)} %x_hbm.5), custom_call_target="tpu_custom_call" | custom-call | flops 1073741824 | bytes 4194304 | tf_op jit(solution)/shard_map/pallas_call | solution.py:357
  4.1 0.0 copy-done
  4.1 0.0 copy-done.1
  4.2 0.0 copy-done.4
  4.2 0.0 copy-done.3
  4.2 0.0 copy-done.2
  4.2 0.8 %shard_map.78 = (f32[416,128]{1,0:T(8,128)S(1)}, f32[416,128]{1,0:T(8,128)S(1)}) custom-call(s32[2]{0:T(128)S(1)} %copy-done.4, s32[2,128]{1,0:T(2,128)S(1)} %copy-done.1, s32[2,128]{1,0:T(2,128)S(1)} %copy-done.1, f32[2,128]{1,0:T(2,128)S(1)} %copy-done.2, f32[2,128]{1,0:T(2,128)S(1)} %copy-done.3, f32[32,128]{1,0:T(8,128)S(1)} %bitcast.3, ...), custom_call_target="tpu_custom_call" | custom-call | tf_op jit(solution)/shard_map/pallas_call | solution.py:371
  5.0 0.5 %collective-permute-start = (f32[416,128]{1,0:T(8,128)S(1)}, f32[416,128]{1,0:T(8,128)S(1)}, u32[]{:S(2)}, u32[]{:S(2)}) collective-permute-start(f32[416,128]{1,0:T(8,128)S(1)} %get-tuple-element.7), channel_id=1, source_target_pairs={{0,1},{1,0},{2,3},{3,2},{4,5},{5,4},{6,7},{7,6},{8,9},{9,8},{10,11... | collective-permute-start | bytes 638984 | tf_op jit(solution)/shard_map/ppermute | solution.py:406
  5.5 1.1 %collective-permute-done = f32[416,128]{1,0:T(8,128)S(1)} collective-permute-done((f32[416,128]{1,0:T(8,128)S(1)}, f32[416,128]{1,0:T(8,128)S(1)}, u32[]{:S(2)}, u32[]{:S(2)}) %collective-permute-start) | collective-permute-done | bytes 213024 | tf_op jit(solution)/shard_map/ppermute | solution.py:406
  6.7 4.1 %collective-permute-start.1 = (f32[208,128]{1,0:T(8,128)S(1)}, f32[208,128]{1,0:T(8,128)S(1)}, u32[]{:S(2)}, u32[]{:S(2)}) collective-permute-start(f32[208,128]{1,0:T(8,128)S(1)} %slice_select_fusion), channel_id=1, source_target_pairs={{0,2},{1,3},{2,0},{3,1},{4,6},{5,7},{6,4},{7,5},{8,10},{9,11},{10,... | collective-permute-start | bytes 319496 | tf_op jit(solution)/shard_map/ppermute | solution.py:406
  10.8 3.5 %collective-permute-done.1 = f32[208,128]{1,0:T(8,128)S(1)} collective-permute-done((f32[208,128]{1,0:T(8,128)S(1)}, f32[208,128]{1,0:T(8,128)S(1)}, u32[]{:S(2)}, u32[]{:S(2)}) %collective-permute-start.1) | collective-permute-done | bytes 106528 | tf_op jit(solution)/shard_map/ppermute | solution.py:406
  14.3 0.5 %collective-permute-start.2 = (f32[208,128]{1,0:T(8,128)S(1)}, f32[208,128]{1,0:T(8,128)S(1)}, u32[]{:S(2)}, u32[]{:S(2)}) collective-permute-start(f32[208,128]{1,0:T(8,128)S(1)} %select_add_fusion), channel_id=1, source_target_pairs={{0,4},{1,5},{2,6},{3,7},{4,0},{5,1},{6,2},{7,3},{8,12},{9,13},{10,... | collective-permute-start | bytes 319496 | tf_op jit(solution)/shard_map/ppermute | solution.py:406
  14.8 4.3 %collective-permute-done.2 = f32[208,128]{1,0:T(8,128)S(1)} collective-permute-done((f32[208,128]{1,0:T(8,128)S(1)}, f32[208,128]{1,0:T(8,128)S(1)}, u32[]{:S(2)}, u32[]{:S(2)}) %collective-permute-start.2) | collective-permute-done | bytes 106528 | tf_op jit(solution)/shard_map/ppermute | solution.py:406
  19.1 3.5 %collective-permute-start.3 = (f32[208,128]{1,0:T(8,128)S(1)}, f32[208,128]{1,0:T(8,128)S(1)}, u32[]{:S(2)}, u32[]{:S(2)}) collective-permute-start(f32[208,128]{1,0:T(8,128)S(1)} %add.14), channel_id=1, source_target_pairs={{0,8},{1,9},{2,10},{3,11},{4,12},{5,13},{6,14},{7,15},{8,0},{9,1},... | collective-permute-start | bytes 319496 | tf_op jit(solution)/shard_map/ppermute | solution.py:406
  22.6 3.2 %collective-permute-done.3 = f32[208,128]{1,0:T(8,128)S(1)} collective-permute-done((f32[208,128]{1,0:T(8,128)S(1)}, f32[208,128]{1,0:T(8,128)S(1)}, u32[]{:S(2)}, u32[]{:S(2)}) %collective-permute-start.3) | collective-permute-done | bytes 106528 | tf_op jit(solution)/shard_map/ppermute | solution.py:406
  25.8 1.6 %collective-permute-start.4 = (f32[208,128]{1,0:T(8,128)S(1)}, f32[208,128]{1,0:T(8,128)S(1)}, u32[]{:S(2)}, u32[]{:S(2)}) collective-permute-start(f32[208,128]{1,0:T(8,128)S(1)} %add.15), channel_id=1, source_target_pairs={{0,2},{1,3},{2,0},{3,1},{4,6},{5,7},{6,4},{7,5},{8,10},{9,11},{10,... | collective-permute-start | bytes 319496 | tf_op jit(solution)/shard_map/ppermute | solution.py:406
  27.4 3.2 %collective-permute-done.4 = f32[208,128]{1,0:T(8,128)S(1)} collective-permute-done((f32[208,128]{1,0:T(8,128)S(1)}, f32[208,128]{1,0:T(8,128)S(1)}, u32[]{:S(2)}, u32[]{:S(2)}) %collective-permute-start.4) | collective-permute-done | bytes 106528 | tf_op jit(solution)/shard_map/ppermute | solution.py:406
  30.6 0.1 collective-permute-start.5
  30.7 1.5 %collective-permute-done.5.other_v = f32[416,128]{1,0:T(8,128)S(1)} collective-permute-done((f32[416,128]{1,0:T(8,128)S(1)}, f32[416,128]{1,0:T(8,128)S(1)}, u32[]{:S(2)}, u32[]{:S(2)}) %collective-permute-start.5) | collective-permute-done | bytes 213024 | tf_op jit(solution)/shard_map/ppermute | solution.py:406
  32.1 14.4 %shard_map.79 = (f32[4096,256]{1,0:T(8,128)}, f32[1,4096]{1,0:T(1,128)}) custom-call(f32[416,128]{1,0:T(8,128)S(1)} %pad_maximum_fusion.mine_v, f32[416,128]{1,0:T(8,128)S(1)} %collective-permute-done.5.other_v, f32[1,4096]{1,0:T(1,128)S(1)} %bitcast.4, f32[4096,256]{1,0:T(8,128)} %x_hbm.5), custom_call_target="tpu_custom_call" | custom-call | tf_op jit(solution)/shard_map/pallas_call | solution.py:388
  (7 shorter events, 0.1 us)
Async XLA Ops:
  0.6 3.5 %copy-start = (f32[4096]{0:T(1024)S(1)}, f32[4096]{0:T(1024)}, u32[]{:S(2)}) copy-start(f32[4096]{0:T(1024)} %param.7) | copy-start | bytes 49156
  0.6 3.5 %copy-start.1 = (s32[2,128]{1,0:T(2,128)S(1)}, s32[2,128]{1,0:T(2,128)}, u32[]{:S(2)}) copy-start(s32[2,128]{1,0:T(2,128)} %rows_v.1) | copy-start | bytes 3076
  0.7 3.5 %copy-start.4 = (s32[2]{0:T(128)S(1)}, s32[2]{0:T(128)}, u32[]{:S(2)}) copy-start(s32[2]{0:T(128)} %owner_s.1) | copy-start | bytes 28
  0.7 3.5 %copy-start.3 = (f32[2,128]{1,0:T(2,128)S(1)}, f32[2,128]{1,0:T(2,128)}, u32[]{:S(2)}) copy-start(f32[2,128]{1,0:T(2,128)} %error_var.1) | copy-start | bytes 3076
  0.7 3.5 %copy-start.2 = (f32[2,128]{1,0:T(2,128)S(1)}, f32[2,128]{1,0:T(2,128)}, u32[]{:S(2)}) copy-start(f32[2,128]{1,0:T(2,128)} %observed.1) | copy-start | bytes 3076
  5.0 1.6 %collective-permute-start = (f32[416,128]{1,0:T(8,128)S(1)}, f32[416,128]{1,0:T(8,128)S(1)}, u32[]{:S(2)}, u32[]{:S(2)}) collective-permute-start(f32[416,128]{1,0:T(8,128)S(1)} %get-tuple-element.7), channel_id=1, source_target_pairs={{0,1},{1,0},{2,3},{3,2},{4,5},{5,4},{6,7},{7,6},{8,9},{9,8},{10,11... | collective-permute-start | bytes 638984 | tf_op jit(solution)/shard_map/ppermute | solution.py:406
  6.7 7.6 %collective-permute-start.1 = (f32[208,128]{1,0:T(8,128)S(1)}, f32[208,128]{1,0:T(8,128)S(1)}, u32[]{:S(2)}, u32[]{:S(2)}) collective-permute-start(f32[208,128]{1,0:T(8,128)S(1)} %slice_select_fusion), channel_id=1, source_target_pairs={{0,2},{1,3},{2,0},{3,1},{4,6},{5,7},{6,4},{7,5},{8,10},{9,11},{10,... | collective-permute-start | bytes 319496 | tf_op jit(solution)/shard_map/ppermute | solution.py:406
  14.3 4.8 %collective-permute-start.2 = (f32[208,128]{1,0:T(8,128)S(1)}, f32[208,128]{1,0:T(8,128)S(1)}, u32[]{:S(2)}, u32[]{:S(2)}) collective-permute-start(f32[208,128]{1,0:T(8,128)S(1)} %select_add_fusion), channel_id=1, source_target_pairs={{0,4},{1,5},{2,6},{3,7},{4,0},{5,1},{6,2},{7,3},{8,12},{9,13},{10,... | collective-permute-start | bytes 319496 | tf_op jit(solution)/shard_map/ppermute | solution.py:406
  19.1 6.7 %collective-permute-start.3 = (f32[208,128]{1,0:T(8,128)S(1)}, f32[208,128]{1,0:T(8,128)S(1)}, u32[]{:S(2)}, u32[]{:S(2)}) collective-permute-start(f32[208,128]{1,0:T(8,128)S(1)} %add.14), channel_id=1, source_target_pairs={{0,8},{1,9},{2,10},{3,11},{4,12},{5,13},{6,14},{7,15},{8,0},{9,1},... | collective-permute-start | bytes 319496 | tf_op jit(solution)/shard_map/ppermute | solution.py:406
  25.8 4.8 %collective-permute-start.4 = (f32[208,128]{1,0:T(8,128)S(1)}, f32[208,128]{1,0:T(8,128)S(1)}, u32[]{:S(2)}, u32[]{:S(2)}) collective-permute-start(f32[208,128]{1,0:T(8,128)S(1)} %add.15), channel_id=1, source_target_pairs={{0,2},{1,3},{2,0},{3,1},{4,6},{5,7},{6,4},{7,5},{8,10},{9,11},{10,... | collective-permute-start | bytes 319496 | tf_op jit(solution)/shard_map/ppermute | solution.py:406
  30.6 1.5 %collective-permute-start.5 = (f32[416,128]{1,0:T(8,128)S(1)}, f32[416,128]{1,0:T(8,128)S(1)}, u32[]{:S(2)}, u32[]{:S(2)}) collective-permute-start(f32[416,128]{1,0:T(8,128)S(1)} %pad_maximum_fusion.mine_v), channel_id=1, source_target_pairs={{0,1},{1,0},{2,3},{3,2},{4,5},{5,4},{6,7},{7,6},{8,9},{9,8},{10,11... | collective-permute-start | bytes 638984 | tf_op jit(solution)/shard_map/ppermute | solution.py:406
where the time goes:
time: 47.1 us; the launch traced here: 46.7 us
  Pallas kernels  18.7 us (40%)
  waiting for transfers between devices  16.7 us (35%)
  starting transfers between devices  10.3 us (22%)
  between operations  0.93 us (2%)
    ppermute x6, waiting for transfers between devices, swap(): return lax.ppermute(value, AXIS, [(i, i ^ mask) for i in range(count)])  16.7 us
    pallas_call x1, Pallas kernels, update(): pl.pallas_call(functools.partial(update_kernel, chunks), out_shape=(jax.S...  14.4 us
    ppermute x6, starting transfers between devices, swap(): return lax.ppermute(value, AXIS, [(i, i ^ mask) for i in range(count)])  10.3 us
    pallas_call x1, Pallas kernels, gram_of(): pl.pallas_call(functools.partial(gram_kernel, chunks), out_shape=jax.Shap...  3.45 us
  transfers between devices with their start and end apart: 6, of which 6 were waited for; matrix products, arithmetic and copies ran while one was open for 0% of the time, Pallas kernels for 0%

commit v1 on v0

--- a/solution.py
+++ b/solution.py
@@ -46,6 +46,18 @@
         return pltpu.make_async_copy(source.at[part], target.at[part], sem.at[i])
 
     return copy
+
+
+def piece_copy(source, target, sem, pieces):
+    def copy(i, at, size):
+        part = pl.ds(at, size)
+        return pltpu.make_async_copy(source.at[part], target.at[part], sem.at[i])
+
+    def every(act):
+        for i, (at, size) in enumerate(pieces):
+            act(copy(i, at, size))
+
+    return copy, every
 
 
 def gram_kernel(chunks, x_hbm, out, x_buf, sem):
@@ -235,11 +247,12 @@
     chunks, mine_v, other_v, mean_v, x_hbm, out_hbm, mean_out, full, x_buf, o_buf, in_sem, out_sem
 ):
     members = x_buf.shape[1]
-    size = x_buf.shape[0] // chunks
-    load = chunk_copy(x_hbm, x_buf, in_sem, chunks)
-    store = chunk_copy(o_buf, out_hbm, out_sem, chunks)
-    for i in range(chunks):
-        load(i).start()
+    rows = x_buf.shape[0]
+    size = rows // chunks
+    pieces = [(0, size // 2)] + [(size // 2 + i * size, size) for i in range(chunks - 1)] + [(rows - size // 2, size // 2)]
+    load, every_load = piece_copy(x_hbm, x_buf, in_sem, pieces)
+    store, every_store = piece_copy(o_buf, out_hbm, out_sem, pieces)
+    every_load(lambda copy: copy.start())
 
     mine = lax.axis_index(AXIS) & 1
     span = PACKED // 2
@@ -274,7 +287,7 @@
     eye = identity(half)
 
     inv_m = factor(eye + dot(first, first, ((1,), (1,))))
-    v_and_f = dot(inv_m, jnp.concatenate([first, innovation(0)], axis=1))
+    v_and_f = dot3(inv_m, jnp.concatenate([first, innovation(0)], axis=1))
     v, f = v_and_f[:, :members], v_and_f[:, members:]
     before = add_up(eye * (g00 + g11))
     after1 = before - add_up(dot3(v, gram) * v)
@@ -286,15 +299,15 @@
     a2 = dot(second, second, ((0,), (0,)))
     square = factor1 * factor1
     k00 = eye + a1[:half, :half] + a2[:half, :half] * square
-    k01 = a1[:half, half:] + a2[:half, half:] * square
+    k10 = a1[half:, :half] + a2[half:, :half] * square
     k11 = eye + a1[half:, half:] + a2[half:, half:] * square
     inv00 = factor(k00)
-    u = dot(inv00, k01)
-    inv11 = factor(k11 - dot(u, u, ((0,), (0,))))
-    inv10 = -dot(inv11, dot(u, inv00, ((0,), (0,))))
+    l10 = dot(k10, inv00, ((1,), (1,)))
+    inv11 = factor(k11 - dot(l10, l10, ((1,), (1,))))
+    inv10 = -dot(inv11, dot(l10, inv00))
     target = dot(second, innov2, ((0,), (0,))) * square
-    y0 = dot(inv00, target[:half, :])
-    y1 = dot(inv11, target[half:, :] - dot(u, y0, ((0,), (0,))))
+    y0 = dot3(inv00, target[:half, :])
+    y1 = dot3(inv11, target[half:, :] - dot3(l10, y0))
     bottom = jnp.concatenate([inv10, inv11], axis=1)
     top_trace = add_up(dot3(inv00, g00) * inv00)
     after2 = top_trace + add_up(dot3(bottom, gram) * bottom)
@@ -311,28 +324,28 @@
     step_line = lax.broadcasted_iota(jnp.int32, (LANES, LANES), 0)
     diagonal = step_line == lax.broadcasted_iota(jnp.int32, (LANES, LANES), 1)
 
-    def apply(i, at):
-        load(i).wait()
+    def apply(i, at, size):
+        load(i, at, size).wait()
         x = x_buf[pl.ds(at, size), :]
         high, low = split(x)
         moved = dot(jnp.concatenate([high, low, high], axis=1), transform, precision=None)
         o_buf[pl.ds(at, size), :] = moved * factor2
-        store(i).start()
+        store(i, at, size).start()
         steps = jnp.sum(x * increment, axis=1, keepdims=True)
         for j in range(0, size, LANES):
             step = jnp.sum(jnp.where(diagonal, steps[j : j + LANES, :], 0.0), axis=0, keepdims=True)
             part = pl.ds(at + j, LANES)
             mean_out[:, part] = mean_v[:, part] + step
 
-    apply(0, 0)
+    apply(0, *pieces[0])
 
     def body(i, _):
-        apply(i, pl.multiple_of(i * size, size))
+        apply(i, pl.multiple_of(i * size - size // 2, size // 2), size)
         return 0
 
     lax.fori_loop(1, chunks, body, 0)
-    for i in range(chunks):
-        store(i).wait()
+    apply(chunks, *pieces[-1])
+    every_store(lambda copy: copy.wait())
 
 
 def spec(space):
@@ -394,8 +407,8 @@
             pltpu.VMEM((PACKED, LANES), F32),
             pltpu.VMEM((rows, members), F32),
             pltpu.VMEM((rows, members), F32),
-            pltpu.SemaphoreType.DMA((chunks,)),
-            pltpu.SemaphoreType.DMA((chunks,)),
+            pltpu.SemaphoreType.DMA((chunks + 1,)),
+            pltpu.SemaphoreType.DMA((chunks + 1,)),
         ],
         compiler_params=params(),
     )(*packed, mean_state.reshape(1, rows), ensemble)

time: 47.1 us -> 46.3 us (0.983); the launches traced: 46.7 us -> 46.7 us
  no operation moved by 1% of the time
where the time goes in v1:
time: 46.3 us; the launch traced here: 46.7 us
  Pallas kernels  18.5 us (40%)
  waiting for transfers between devices  17.1 us (37%)
  starting transfers between devices  9.95 us (21%)
  between operations  0.93 us (2%)
    ppermute x6, waiting for transfers between devices, swap(): return lax.ppermute(value, AXIS, [(i, i ^ mask) for i in range(count)])  17.1 us
    pallas_call x1, Pallas kernels, update(): pl.pallas_call(functools.partial(update_kernel, chunks), out_shape=(jax.S...  14.2 us
    ppermute x6, starting transfers between devices, swap(): return lax.ppermute(value, AXIS, [(i, i ^ mask) for i in range(count)])  9.95 us
    pallas_call x1, Pallas kernels, gram_of(): pl.pallas_call(functools.partial(gram_kernel, chunks), out_shape=jax.Shap...  3.45 us
  transfers between devices with their start and end apart: 6, of which 6 were waited for; matrix products, arithmetic and copies ran while one was open for 0% of the time, Pallas kernels for 0%

profile of v1, /device:TPU:0, one launch (start us, length us, event | category | flops | bytes accessed | tf_op | source)
XLA Modules:
  0.0 46.7 jit_solution(11555587897878489418)
XLA Ops:
  0.6 0.0 copy-start
  0.6 0.0 copy-start.1
  0.7 0.0 copy-start.4
  0.7 0.0 copy-start.3
  0.7 0.0 copy-start.2
  0.7 3.4 %shard_map.77.gram = f32[320,128]{1,0:T(8,128)S(1)} custom-call(f32[4096,256]{1,0:T(8,128)} %x_hbm.5), custom_call_target="tpu_custom_call" | custom-call | flops 1073741824 | bytes 4194304 | tf_op jit(solution)/shard_map/pallas_call | solution.py:370
  4.1 0.0 copy-done
  4.1 0.0 copy-done.1
  4.2 0.0 copy-done.4
  4.2 0.0 copy-done.3
  4.2 0.0 copy-done.2
  4.2 0.8 %shard_map.78 = (f32[416,128]{1,0:T(8,128)S(1)}, f32[416,128]{1,0:T(8,128)S(1)}) custom-call(s32[2]{0:T(128)S(1)} %copy-done.4, s32[2,128]{1,0:T(2,128)S(1)} %copy-done.1, s32[2,128]{1,0:T(2,128)S(1)} %copy-done.1, f32[2,128]{1,0:T(2,128)S(1)} %copy-done.2, f32[2,128]{1,0:T(2,128)S(1)} %copy-done.3, f32[32,128]{1,0:T(8,128)S(1)} %bitcast.3, ...), custom_call_target="tpu_custom_call" | custom-call | tf_op jit(solution)/shard_map/pallas_call | solution.py:384
  5.0 0.5 %collective-permute-start = (f32[416,128]{1,0:T(8,128)S(1)}, f32[416,128]{1,0:T(8,128)S(1)}, u32[]{:S(2)}, u32[]{:S(2)}) collective-permute-start(f32[416,128]{1,0:T(8,128)S(1)} %get-tuple-element.7), channel_id=1, source_target_pairs={{0,1},{1,0},{2,3},{3,2},{4,5},{5,4},{6,7},{7,6},{8,9},{9,8},{10,11... | collective-permute-start | bytes 638984 | tf_op jit(solution)/shard_map/ppermute | solution.py:419
  5.5 1.1 %collective-permute-done = f32[416,128]{1,0:T(8,128)S(1)} collective-permute-done((f32[416,128]{1,0:T(8,128)S(1)}, f32[416,128]{1,0:T(8,128)S(1)}, u32[]{:S(2)}, u32[]{:S(2)}) %collective-permute-start) | collective-permute-done | bytes 213024 | tf_op jit(solution)/shard_map/ppermute | solution.py:419
  6.7 3.0 %collective-permute-start.1 = (f32[208,128]{1,0:T(8,128)S(1)}, f32[208,128]{1,0:T(8,128)S(1)}, u32[]{:S(2)}, u32[]{:S(2)}) collective-permute-start(f32[208,128]{1,0:T(8,128)S(1)} %slice_select_fusion), channel_id=1, source_target_pairs={{0,2},{1,3},{2,0},{3,1},{4,6},{5,7},{6,4},{7,5},{8,10},{9,11},{10,... | collective-permute-start | bytes 319496 | tf_op jit(solution)/shard_map/ppermute | solution.py:419
  9.6 3.3 %collective-permute-done.1 = f32[208,128]{1,0:T(8,128)S(1)} collective-permute-done((f32[208,128]{1,0:T(8,128)S(1)}, f32[208,128]{1,0:T(8,128)S(1)}, u32[]{:S(2)}, u32[]{:S(2)}) %collective-permute-start.1) | collective-permute-done | bytes 106528 | tf_op jit(solution)/shard_map/ppermute | solution.py:419
  12.9 1.9 %collective-permute-start.2 = (f32[208,128]{1,0:T(8,128)S(1)}, f32[208,128]{1,0:T(8,128)S(1)}, u32[]{:S(2)}, u32[]{:S(2)}) collective-permute-start(f32[208,128]{1,0:T(8,128)S(1)} %select_add_fusion), channel_id=1, source_target_pairs={{0,4},{1,5},{2,6},{3,7},{4,0},{5,1},{6,2},{7,3},{8,12},{9,13},{10,... | collective-permute-start | bytes 319496 | tf_op jit(solution)/shard_map/ppermute | solution.py:419
  14.8 2.9 %collective-permute-done.2 = f32[208,128]{1,0:T(8,128)S(1)} collective-permute-done((f32[208,128]{1,0:T(8,128)S(1)}, f32[208,128]{1,0:T(8,128)S(1)}, u32[]{:S(2)}, u32[]{:S(2)}) %collective-permute-start.2) | collective-permute-done | bytes 106528 | tf_op jit(solution)/shard_map/ppermute | solution.py:419
  17.7 4.4 %collective-permute-start.3 = (f32[208,128]{1,0:T(8,128)S(1)}, f32[208,128]{1,0:T(8,128)S(1)}, u32[]{:S(2)}, u32[]{:S(2)}) collective-permute-start(f32[208,128]{1,0:T(8,128)S(1)} %add.14), channel_id=1, source_target_pairs={{0,8},{1,9},{2,10},{3,11},{4,12},{5,13},{6,14},{7,15},{8,0},{9,1},... | collective-permute-start | bytes 319496 | tf_op jit(solution)/shard_map/ppermute | solution.py:419
  22.1 3.8 %collective-permute-done.3 = f32[208,128]{1,0:T(8,128)S(1)} collective-permute-done((f32[208,128]{1,0:T(8,128)S(1)}, f32[208,128]{1,0:T(8,128)S(1)}, u32[]{:S(2)}, u32[]{:S(2)}) %collective-permute-start.3) | collective-permute-done | bytes 106528 | tf_op jit(solution)/shard_map/ppermute | solution.py:419
  25.9 0.2 collective-permute-start.4
  26.1 4.6 %collective-permute-done.4 = f32[208,128]{1,0:T(8,128)S(1)} collective-permute-done((f32[208,128]{1,0:T(8,128)S(1)}, f32[208,128]{1,0:T(8,128)S(1)}, u32[]{:S(2)}, u32[]{:S(2)}) %collective-permute-start.4) | collective-permute-done | bytes 106528 | tf_op jit(solution)/shard_map/ppermute | solution.py:419
  30.7 0.1 collective-permute-start.5
  30.8 1.5 %collective-permute-done.5.other_v = f32[416,128]{1,0:T(8,128)S(1)} collective-permute-done((f32[416,128]{1,0:T(8,128)S(1)}, f32[416,128]{1,0:T(8,128)S(1)}, u32[]{:S(2)}, u32[]{:S(2)}) %collective-permute-start.5) | collective-permute-done | bytes 213024 | tf_op jit(solution)/shard_map/ppermute | solution.py:419
  32.3 14.2 %shard_map.79 = (f32[4096,256]{1,0:T(8,128)}, f32[1,4096]{1,0:T(1,128)}) custom-call(f32[416,128]{1,0:T(8,128)S(1)} %pad_maximum_fusion.mine_v, f32[416,128]{1,0:T(8,128)S(1)} %collective-permute-done.5.other_v, f32[1,4096]{1,0:T(1,128)S(1)} %bitcast.4, f32[4096,256]{1,0:T(8,128)} %x_hbm.5), custom_call_target="tpu_custom_call" | custom-call | tf_op jit(solution)/shard_map/pallas_call | solution.py:401
  (7 shorter events, 0.1 us)
Async XLA Ops:
  0.6 3.5 %copy-start = (f32[4096]{0:T(1024)S(1)}, f32[4096]{0:T(1024)}, u32[]{:S(2)}) copy-start(f32[4096]{0:T(1024)} %param.7) | copy-start | bytes 49156
  0.6 3.5 %copy-start.1 = (s32[2,128]{1,0:T(2,128)S(1)}, s32[2,128]{1,0:T(2,128)}, u32[]{:S(2)}) copy-start(s32[2,128]{1,0:T(2,128)} %rows_v.1) | copy-start | bytes 3076
  0.7 3.5 %copy-start.4 = (s32[2]{0:T(128)S(1)}, s32[2]{0:T(128)}, u32[]{:S(2)}) copy-start(s32[2]{0:T(128)} %owner_s.1) | copy-start | bytes 28
  0.7 3.5 %copy-start.3 = (f32[2,128]{1,0:T(2,128)S(1)}, f32[2,128]{1,0:T(2,128)}, u32[]{:S(2)}) copy-start(f32[2,128]{1,0:T(2,128)} %error_var.1) | copy-start | bytes 3076
  0.7 3.5 %copy-start.2 = (f32[2,128]{1,0:T(2,128)S(1)}, f32[2,128]{1,0:T(2,128)}, u32[]{:S(2)}) copy-start(f32[2,128]{1,0:T(2,128)} %observed.1) | copy-start | bytes 3076
  5.0 1.6 %collective-permute-start = (f32[416,128]{1,0:T(8,128)S(1)}, f32[416,128]{1,0:T(8,128)S(1)}, u32[]{:S(2)}, u32[]{:S(2)}) collective-permute-start(f32[416,128]{1,0:T(8,128)S(1)} %get-tuple-element.7), channel_id=1, source_target_pairs={{0,1},{1,0},{2,3},{3,2},{4,5},{5,4},{6,7},{7,6},{8,9},{9,8},{10,11... | collective-permute-start | bytes 638984 | tf_op jit(solution)/shard_map/ppermute | solution.py:419
  6.7 6.2 %collective-permute-start.1 = (f32[208,128]{1,0:T(8,128)S(1)}, f32[208,128]{1,0:T(8,128)S(1)}, u32[]{:S(2)}, u32[]{:S(2)}) collective-permute-start(f32[208,128]{1,0:T(8,128)S(1)} %slice_select_fusion), channel_id=1, source_target_pairs={{0,2},{1,3},{2,0},{3,1},{4,6},{5,7},{6,4},{7,5},{8,10},{9,11},{10,... | collective-permute-start | bytes 319496 | tf_op jit(solution)/shard_map/ppermute | solution.py:419
  12.9 4.8 %collective-permute-start.2 = (f32[208,128]{1,0:T(8,128)S(1)}, f32[208,128]{1,0:T(8,128)S(1)}, u32[]{:S(2)}, u32[]{:S(2)}) collective-permute-start(f32[208,128]{1,0:T(8,128)S(1)} %select_add_fusion), channel_id=1, source_target_pairs={{0,4},{1,5},{2,6},{3,7},{4,0},{5,1},{6,2},{7,3},{8,12},{9,13},{10,... | collective-permute-start | bytes 319496 | tf_op jit(solution)/shard_map/ppermute | solution.py:419
  17.7 8.2 %collective-permute-start.3 = (f32[208,128]{1,0:T(8,128)S(1)}, f32[208,128]{1,0:T(8,128)S(1)}, u32[]{:S(2)}, u32[]{:S(2)}) collective-permute-start(f32[208,128]{1,0:T(8,128)S(1)} %add.14), channel_id=1, source_target_pairs={{0,8},{1,9},{2,10},{3,11},{4,12},{5,13},{6,14},{7,15},{8,0},{9,1},... | collective-permute-start | bytes 319496 | tf_op jit(solution)/shard_map/ppermute | solution.py:419
  25.9 4.8 %collective-permute-start.4 = (f32[208,128]{1,0:T(8,128)S(1)}, f32[208,128]{1,0:T(8,128)S(1)}, u32[]{:S(2)}, u32[]{:S(2)}) collective-permute-start(f32[208,128]{1,0:T(8,128)S(1)} %add.15), channel_id=1, source_target_pairs={{0,2},{1,3},{2,0},{3,1},{4,6},{5,7},{6,4},{7,5},{8,10},{9,11},{10,... | collective-permute-start | bytes 319496 | tf_op jit(solution)/shard_map/ppermute | solution.py:419
  30.7 1.5 %collective-permute-start.5 = (f32[416,128]{1,0:T(8,128)S(1)}, f32[416,128]{1,0:T(8,128)S(1)}, u32[]{:S(2)}, u32[]{:S(2)}) collective-permute-start(f32[416,128]{1,0:T(8,128)S(1)} %pad_maximum_fusion.mine_v), channel_id=1, source_target_pairs={{0,1},{1,0},{2,3},{3,2},{4,5},{5,4},{6,7},{7,6},{8,9},{9,8},{10,11... | collective-permute-start | bytes 638984 | tf_op jit(solution)/shard_map/ppermute | solution.py:419

commit v2 on v1

--- a/solution.py
+++ b/solution.py
@@ -38,16 +38,6 @@
     return high, (x - high.astype(F32)).astype(BF16)
 
 
-def chunk_copy(source, target, sem, chunks):
-    size = source.shape[0] // chunks
-
-    def copy(i):
-        part = pl.ds(i * size, size)
-        return pltpu.make_async_copy(source.at[part], target.at[part], sem.at[i])
-
-    return copy
-
-
 def piece_copy(source, target, sem, pieces):
     def copy(i, at, size):
         part = pl.ds(at, size)
@@ -60,17 +50,17 @@
     return copy, every
 
 
-def gram_kernel(chunks, x_hbm, out, x_buf, sem):
-    members = x_buf.shape[1]
-    size = x_buf.shape[0] // chunks
+def gram_kernel(x_hbm, out, x_buf, sem):
+    rows, members = x_buf.shape
     half = members // 2
-    copy = chunk_copy(x_hbm, x_buf, sem, chunks)
-    for i in range(chunks):
-        copy(i).start()
+    quarter = rows // 4
+    pieces = [(0, quarter), (quarter, quarter), (2 * quarter, rows - 2 * quarter)]
+    load, every_load = piece_copy(x_hbm, x_buf, sem, pieces)
+    every_load(lambda copy: copy.start())
     total = None
-    for i in range(chunks):
-        copy(i).wait()
-        high, low = split(x_buf[i * size : (i + 1) * size, :])
+    for i, (at, size) in enumerate(pieces):
+        load(i, at, size).wait()
+        high, low = split(x_buf[at : at + size, :])
         part = dot(high, jnp.concatenate([high, low], axis=1), ((0,), (0,)), None)
         total = part if total is None else total + part
     cross = total[:, members:]
@@ -95,24 +85,19 @@
     full[G00:, :] = gram[...]
     full[INNOV : INNOV + 2 * OBS // INNOV_LANES, :INNOV_LANES] = jnp.zeros((2 * OBS // INNOV_LANES, INNOV_LANES), F32)
     lane = lax.broadcasted_iota(jnp.int32, (OBS, LANES), 1)
-    lines = mean_v.shape[0]
-    fetches = OBS // lines
 
     for k, left, right in ((0, A0, A1), (1, B0, B1)):
 
         @pl.when(owner_s[k] == me)
         def _(k=k, left=left, right=right):
+            for o in range(OBS):
+                pltpu.make_async_copy(
+                    x_hbm.at[pl.ds(rows_s[k, o], 1)], picked.at[k, pl.ds(o, 1)], sem.at[k]
+                ).start()
             index = column(rows_v[k : k + 1, :].astype(F32)).astype(jnp.int32) - lane
-
-            def look(r, prior):
-                for j in range(fetches):
-                    o = r * fetches + j
-                    pltpu.make_async_copy(
-                        x_hbm.at[pl.ds(rows_s[k, o], 1)], picked.at[k, pl.ds(o, 1)], sem.at[k]
-                    ).start()
-                return prior + jnp.where(index == r * LANES, mean_v[pl.ds(r, 1), :], 0.0)
-
-            prior = lax.fori_loop(0, lines, look, jnp.zeros((OBS, LANES), F32), unroll=8)
+            prior = jnp.zeros((OBS, LANES), F32)
+            for r in range(mean_v.shape[0]):
+                prior = prior + jnp.where(index == r * LANES, mean_v[r : r + 1, :], 0.0)
             prior = jnp.sum(prior.T, axis=0, keepdims=True)
             scale = lax.rsqrt(error_var[k : k + 1, :] * (members - 1.0))
             innov = scale * (observed[k : k + 1, :] - prior)
@@ -366,13 +351,12 @@
 
 def gram_of(ensemble):
     rows, members = ensemble.shape
-    chunks = 4
     return pl.pallas_call(
-        functools.partial(gram_kernel, chunks),
+        gram_kernel,
         out_shape=jax.ShapeDtypeStruct((PACKED - G00, LANES), F32),
         in_specs=[spec(pltpu.HBM)],
         out_specs=spec(pltpu.VMEM),
-        scratch_shapes=[pltpu.VMEM((rows, members), F32), pltpu.SemaphoreType.DMA((chunks,))],
+        scratch_shapes=[pltpu.VMEM((rows, members), F32), pltpu.SemaphoreType.DMA((3,))],
         cost_estimate=cost(4 * rows * members * members, 4 * rows * members),
         compiler_params=params(),
     )(ensemble)

time: 46.3 us -> 46.7 us (level)
  waiting for transfers between devices: 17.1 us -> 18.6 us
  starting transfers between devices: 9.95 us -> 8.78 us
    ppermute x6, waiting for transfers between devices: 17.1 us -> 18.6 us  [swap(): return lax.ppermute(value, AXIS, [(i, i ^ mask) for i in range(count)])]
    ppermute x6, starting transfers between devices: 9.95 us -> 8.78 us  [swap(): return lax.ppermute(value, AXIS, [(i, i ^ mask) for i in range(count)])]
where the time goes in v2:
time: 46.7 us
  waiting for transfers between devices  18.6 us (40%)
  Pallas kernels  18.3 us (39%)
  starting transfers between devices  8.78 us (19%)
  between operations  0.93 us (2%)
    ppermute x6, waiting for transfers between devices, swap(): return lax.ppermute(value, AXIS, [(i, i ^ mask) for i in range(count)])  18.6 us
    pallas_call x1, Pallas kernels, update(): pl.pallas_call(functools.partial(update_kernel, chunks), out_shape=(jax.S...  14.2 us
    ppermute x6, starting transfers between devices, swap(): return lax.ppermute(value, AXIS, [(i, i ^ mask) for i in range(count)])  8.78 us
    pallas_call x1, Pallas kernels, gram_of(): pl.pallas_call(gram_kernel, out_shape=jax.ShapeDtypeStruct((PACKED - G00,...  3.23 us
  transfers between devices with their start and end apart: 6, of which 6 were waited for; matrix products, arithmetic and copies ran while one was open for 0% of the time, Pallas kernels for 0%

profile of v2, /device:TPU:0, one launch (start us, length us, event | category | flops | bytes accessed | tf_op | source)
XLA Modules:
  0.0 46.7 jit_solution(1148452785020410713)
XLA Ops:
  0.6 0.0 copy-start
  0.6 0.0 copy-start.1
  0.7 0.0 copy-start.4
  0.7 0.0 copy-start.3
  0.7 0.0 copy-start.2
  0.7 3.2 %shard_map.77.gram = f32[320,128]{1,0:T(8,128)S(1)} custom-call(f32[4096,256]{1,0:T(8,128)} %x_hbm.5), custom_call_target="tpu_custom_call" | custom-call | flops 1073741824 | bytes 4194304 | tf_op jit(solution)/shard_map/pallas_call | solution.py:354
  3.9 0.0 copy-done
  3.9 0.0 copy-done.1
  3.9 0.0 copy-done.4
  4.0 0.0 copy-done.3
  4.0 0.0 copy-done.2
  4.0 0.8 %shard_map.78 = (f32[416,128]{1,0:T(8,128)S(1)}, f32[416,128]{1,0:T(8,128)S(1)}) custom-call(s32[2]{0:T(128)S(1)} %copy-done.4, s32[2,128]{1,0:T(2,128)S(1)} %copy-done.1, s32[2,128]{1,0:T(2,128)S(1)} %copy-done.1, f32[2,128]{1,0:T(2,128)S(1)} %copy-done.2, f32[2,128]{1,0:T(2,128)S(1)} %copy-done.3, f32[32,128]{1,0:T(8,128)S(1)} %bitcast.3, ...), custom_call_target="tpu_custom_call" | custom-call | tf_op jit(solution)/shard_map/pallas_call | solution.py:368
  4.8 0.5 %collective-permute-start = (f32[416,128]{1,0:T(8,128)S(1)}, f32[416,128]{1,0:T(8,128)S(1)}, u32[]{:S(2)}, u32[]{:S(2)}) collective-permute-start(f32[416,128]{1,0:T(8,128)S(1)} %get-tuple-element.7), channel_id=1, source_target_pairs={{0,1},{1,0},{2,3},{3,2},{4,5},{5,4},{6,7},{7,6},{8,9},{9,8},{10,11... | collective-permute-start | bytes 638984 | tf_op jit(solution)/shard_map/ppermute | solution.py:403
  5.3 1.1 %collective-permute-done = f32[416,128]{1,0:T(8,128)S(1)} collective-permute-done((f32[416,128]{1,0:T(8,128)S(1)}, f32[416,128]{1,0:T(8,128)S(1)}, u32[]{:S(2)}, u32[]{:S(2)}) %collective-permute-start) | collective-permute-done | bytes 213024 | tf_op jit(solution)/shard_map/ppermute | solution.py:403
  6.5 4.6 %collective-permute-start.1 = (f32[208,128]{1,0:T(8,128)S(1)}, f32[208,128]{1,0:T(8,128)S(1)}, u32[]{:S(2)}, u32[]{:S(2)}) collective-permute-start(f32[208,128]{1,0:T(8,128)S(1)} %slice_select_fusion), channel_id=1, source_target_pairs={{0,2},{1,3},{2,0},{3,1},{4,6},{5,7},{6,4},{7,5},{8,10},{9,11},{10,... | collective-permute-start | bytes 319496 | tf_op jit(solution)/shard_map/ppermute | solution.py:403
  11.0 3.3 %collective-permute-done.1 = f32[208,128]{1,0:T(8,128)S(1)} collective-permute-done((f32[208,128]{1,0:T(8,128)S(1)}, f32[208,128]{1,0:T(8,128)S(1)}, u32[]{:S(2)}, u32[]{:S(2)}) %collective-permute-start.1) | collective-permute-done | bytes 106528 | tf_op jit(solution)/shard_map/ppermute | solution.py:403
  14.3 0.2 collective-permute-start.2
  14.6 4.5 %collective-permute-done.2 = f32[208,128]{1,0:T(8,128)S(1)} collective-permute-done((f32[208,128]{1,0:T(8,128)S(1)}, f32[208,128]{1,0:T(8,128)S(1)}, u32[]{:S(2)}, u32[]{:S(2)}) %collective-permute-start.2) | collective-permute-done | bytes 106528 | tf_op jit(solution)/shard_map/ppermute | solution.py:403
  19.1 2.1 %collective-permute-start.3 = (f32[208,128]{1,0:T(8,128)S(1)}, f32[208,128]{1,0:T(8,128)S(1)}, u32[]{:S(2)}, u32[]{:S(2)}) collective-permute-start(f32[208,128]{1,0:T(8,128)S(1)} %add.14), channel_id=1, source_target_pairs={{0,8},{1,9},{2,10},{3,11},{4,12},{5,13},{6,14},{7,15},{8,0},{9,1},... | collective-permute-start | bytes 319496 | tf_op jit(solution)/shard_map/ppermute | solution.py:403
  21.3 4.7 %collective-permute-done.3 = f32[208,128]{1,0:T(8,128)S(1)} collective-permute-done((f32[208,128]{1,0:T(8,128)S(1)}, f32[208,128]{1,0:T(8,128)S(1)}, u32[]{:S(2)}, u32[]{:S(2)}) %collective-permute-start.3) | collective-permute-done | bytes 106528 | tf_op jit(solution)/shard_map/ppermute | solution.py:403
  25.9 1.2 %collective-permute-start.4 = (f32[208,128]{1,0:T(8,128)S(1)}, f32[208,128]{1,0:T(8,128)S(1)}, u32[]{:S(2)}, u32[]{:S(2)}) collective-permute-start(f32[208,128]{1,0:T(8,128)S(1)} %add.15), channel_id=1, source_target_pairs={{0,2},{1,3},{2,0},{3,1},{4,6},{5,7},{6,4},{7,5},{8,10},{9,11},{10,... | collective-permute-start | bytes 319496 | tf_op jit(solution)/shard_map/ppermute | solution.py:403
  27.2 3.5 %collective-permute-done.4 = f32[208,128]{1,0:T(8,128)S(1)} collective-permute-done((f32[208,128]{1,0:T(8,128)S(1)}, f32[208,128]{1,0:T(8,128)S(1)}, u32[]{:S(2)}, u32[]{:S(2)}) %collective-permute-start.4) | collective-permute-done | bytes 106528 | tf_op jit(solution)/shard_map/ppermute | solution.py:403
  30.8 0.1 collective-permute-start.5
  30.8 1.5 %collective-permute-done.5.other_v = f32[416,128]{1,0:T(8,128)S(1)} collective-permute-done((f32[416,128]{1,0:T(8,128)S(1)}, f32[416,128]{1,0:T(8,128)S(1)}, u32[]{:S(2)}, u32[]{:S(2)}) %collective-permute-start.5) | collective-permute-done | bytes 213024 | tf_op jit(solution)/shard_map/ppermute | solution.py:403
  32.3 14.2 %shard_map.79 = (f32[4096,256]{1,0:T(8,128)}, f32[1,4096]{1,0:T(1,128)}) custom-call(f32[416,128]{1,0:T(8,128)S(1)} %pad_maximum_fusion.mine_v, f32[416,128]{1,0:T(8,128)S(1)} %collective-permute-done.5.other_v, f32[1,4096]{1,0:T(1,128)S(1)} %bitcast.4, f32[4096,256]{1,0:T(8,128)} %x_hbm.5), custom_call_target="tpu_custom_call" | custom-call | tf_op jit(solution)/shard_map/pallas_call | solution.py:385
  (7 shorter events, 0.1 us)
Async XLA Ops:
  0.6 3.3 %copy-start = (f32[4096]{0:T(1024)S(1)}, f32[4096]{0:T(1024)}, u32[]{:S(2)}) copy-start(f32[4096]{0:T(1024)} %param.7) | copy-start | bytes 49156
  0.6 3.3 %copy-start.1 = (s32[2,128]{1,0:T(2,128)S(1)}, s32[2,128]{1,0:T(2,128)}, u32[]{:S(2)}) copy-start(s32[2,128]{1,0:T(2,128)} %rows_v.1) | copy-start | bytes 3076
  0.7 3.3 %copy-start.4 = (s32[2]{0:T(128)S(1)}, s32[2]{0:T(128)}, u32[]{:S(2)}) copy-start(s32[2]{0:T(128)} %owner_s.1) | copy-start | bytes 28
  0.7 3.3 %copy-start.3 = (f32[2,128]{1,0:T(2,128)S(1)}, f32[2,128]{1,0:T(2,128)}, u32[]{:S(2)}) copy-start(f32[2,128]{1,0:T(2,128)} %error_var.1) | copy-start | bytes 3076
  0.7 3.3 %copy-start.2 = (f32[2,128]{1,0:T(2,128)S(1)}, f32[2,128]{1,0:T(2,128)}, u32[]{:S(2)}) copy-start(f32[2,128]{1,0:T(2,128)} %observed.1) | copy-start | bytes 3076
  4.8 1.6 %collective-permute-start = (f32[416,128]{1,0:T(8,128)S(1)}, f32[416,128]{1,0:T(8,128)S(1)}, u32[]{:S(2)}, u32[]{:S(2)}) collective-permute-start(f32[416,128]{1,0:T(8,128)S(1)} %get-tuple-element.7), channel_id=1, source_target_pairs={{0,1},{1,0},{2,3},{3,2},{4,5},{5,4},{6,7},{7,6},{8,9},{9,8},{10,11... | collective-permute-start | bytes 638984 | tf_op jit(solution)/shard_map/ppermute | solution.py:403
  6.5 7.9 %collective-permute-start.1 = (f32[208,128]{1,0:T(8,128)S(1)}, f32[208,128]{1,0:T(8,128)S(1)}, u32[]{:S(2)}, u32[]{:S(2)}) collective-permute-start(f32[208,128]{1,0:T(8,128)S(1)} %slice_select_fusion), channel_id=1, source_target_pairs={{0,2},{1,3},{2,0},{3,1},{4,6},{5,7},{6,4},{7,5},{8,10},{9,11},{10,... | collective-permute-start | bytes 319496 | tf_op jit(solution)/shard_map/ppermute | solution.py:403
  14.3 4.8 %collective-permute-start.2 = (f32[208,128]{1,0:T(8,128)S(1)}, f32[208,128]{1,0:T(8,128)S(1)}, u32[]{:S(2)}, u32[]{:S(2)}) collective-permute-start(f32[208,128]{1,0:T(8,128)S(1)} %select_add_fusion), channel_id=1, source_target_pairs={{0,4},{1,5},{2,6},{3,7},{4,0},{5,1},{6,2},{7,3},{8,12},{9,13},{10,... | collective-permute-start | bytes 319496 | tf_op jit(solution)/shard_map/ppermute | solution.py:403
  19.1 6.8 %collective-permute-start.3 = (f32[208,128]{1,0:T(8,128)S(1)}, f32[208,128]{1,0:T(8,128)S(1)}, u32[]{:S(2)}, u32[]{:S(2)}) collective-permute-start(f32[208,128]{1,0:T(8,128)S(1)} %add.14), channel_id=1, source_target_pairs={{0,8},{1,9},{2,10},{3,11},{4,12},{5,13},{6,14},{7,15},{8,0},{9,1},... | collective-permute-start | bytes 319496 | tf_op jit(solution)/shard_map/ppermute | solution.py:403
  25.9 4.8 %collective-permute-start.4 = (f32[208,128]{1,0:T(8,128)S(1)}, f32[208,128]{1,0:T(8,128)S(1)}, u32[]{:S(2)}, u32[]{:S(2)}) collective-permute-start(f32[208,128]{1,0:T(8,128)S(1)} %add.15), channel_id=1, source_target_pairs={{0,2},{1,3},{2,0},{3,1},{4,6},{5,7},{6,4},{7,5},{8,10},{9,11},{10,... | collective-permute-start | bytes 319496 | tf_op jit(solution)/shard_map/ppermute | solution.py:403
  30.8 1.5 %collective-permute-start.5 = (f32[416,128]{1,0:T(8,128)S(1)}, f32[416,128]{1,0:T(8,128)S(1)}, u32[]{:S(2)}, u32[]{:S(2)}) collective-permute-start(f32[416,128]{1,0:T(8,128)S(1)} %pad_maximum_fusion.mine_v), channel_id=1, source_target_pairs={{0,1},{1,0},{2,3},{3,2},{4,5},{5,4},{6,7},{7,6},{8,9},{9,8},{10,11... | collective-permute-start | bytes 638984 | tf_op jit(solution)/shard_map/ppermute | solution.py:403

commit v3 on v2

--- a/solution.py
+++ b/solution.py
@@ -93,7 +93,7 @@
             for o in range(OBS):
                 pltpu.make_async_copy(
                     x_hbm.at[pl.ds(rows_s[k, o], 1)], picked.at[k, pl.ds(o, 1)], sem.at[k]
-                ).start()
+                ).start(priority=o % 2)
             index = column(rows_v[k : k + 1, :].astype(F32)).astype(jnp.int32) - lane
             prior = jnp.zeros((OBS, LANES), F32)
             for r in range(mean_v.shape[0]):
@@ -304,17 +304,20 @@
     turned = jnp.concatenate(
         [jnp.concatenate([inv00.T, inv10.T], axis=1), jnp.concatenate([jnp.zeros_like(inv00), inv11.T], axis=1)], axis=0
     )
-    high, low = split(turned)
-    transform = jnp.concatenate([high, high, low], axis=0)
+
+    def stacked(x):
+        high, low = split(x)
+        return jnp.concatenate([high, high, low], axis=0)
+
     step_line = lax.broadcasted_iota(jnp.int32, (LANES, LANES), 0)
     diagonal = step_line == lax.broadcasted_iota(jnp.int32, (LANES, LANES), 1)
 
-    def apply(i, at, size):
+    def apply(i, at, size, transform, scale):
         load(i, at, size).wait()
         x = x_buf[pl.ds(at, size), :]
         high, low = split(x)
         moved = dot(jnp.concatenate([high, low, high], axis=1), transform, precision=None)
-        o_buf[pl.ds(at, size), :] = moved * factor2
+        o_buf[pl.ds(at, size), :] = moved if scale is None else moved * scale
         store(i, at, size).start()
         steps = jnp.sum(x * increment, axis=1, keepdims=True)
         for j in range(0, size, LANES):
@@ -322,14 +325,15 @@
             part = pl.ds(at + j, LANES)
             mean_out[:, part] = mean_v[:, part] + step
 
-    apply(0, *pieces[0])
+    apply(0, *pieces[0], stacked(turned), factor2)
+    scaled = stacked(turned * factor2)
 
     def body(i, _):
-        apply(i, pl.multiple_of(i * size - size // 2, size // 2), size)
+        apply(i, pl.multiple_of(i * size - size // 2, size // 2), size, scaled, None)
         return 0
 
     lax.fori_loop(1, chunks, body, 0)
-    apply(chunks, *pieces[-1])
+    apply(chunks, *pieces[-1], scaled, None)
     every_store(lambda copy: copy.wait())
 
 

time: 46.7 us -> 46.5 us (level)
  waiting for transfers between devices: 18.6 us -> 17.7 us
  starting transfers between devices: 8.78 us -> 9.51 us
    ppermute x6, waiting for transfers between devices: 18.6 us -> 17.7 us  [swap(): return lax.ppermute(value, AXIS, [(i, i ^ mask) for i in range(count)])]
    ppermute x6, starting transfers between devices: 8.78 us -> 9.51 us  [swap(): return lax.ppermute(value, AXIS, [(i, i ^ mask) for i in range(count)])]
where the time goes in v3:
time: 46.5 us
  Pallas kernels  18.2 us (39%)
  waiting for transfers between devices  17.7 us (38%)
  starting transfers between devices  9.51 us (20%)
  between operations  0.93 us (2%)
    ppermute x6, waiting for transfers between devices, swap(): return lax.ppermute(value, AXIS, [(i, i ^ mask) for i in range(count)])  17.7 us
    pallas_call x1, Pallas kernels, update(): pl.pallas_call(functools.partial(update_kernel, chunks), out_shape=(jax.S...  14.2 us
    ppermute x6, starting transfers between devices, swap(): return lax.ppermute(value, AXIS, [(i, i ^ mask) for i in range(count)])  9.51 us
    pallas_call x1, Pallas kernels, gram_of(): pl.pallas_call(gram_kernel, out_shape=jax.ShapeDtypeStruct((PACKED - G00,...  3.23 us
  transfers between devices with their start and end apart: 6, of which 6 were waited for; matrix products, arithmetic and copies ran while one was open for 0% of the time, Pallas kernels for 0%

profile of v3, /device:TPU:0, one launch (start us, length us, event | category | flops | bytes accessed | tf_op | source)
XLA Modules:
  0.0 46.5 jit_solution(5432838561411503636)
XLA Ops:
  0.6 0.0 copy-start
  0.6 0.0 copy-start.1
  0.7 0.0 copy-start.4
  0.7 0.0 copy-start.3
  0.7 0.0 copy-start.2
  0.7 3.2 %shard_map.77.gram = f32[320,128]{1,0:T(8,128)S(1)} custom-call(f32[4096,256]{1,0:T(8,128)} %x_hbm.5), custom_call_target="tpu_custom_call" | custom-call | flops 1073741824 | bytes 4194304 | tf_op jit(solution)/shard_map/pallas_call | solution.py:358
  3.9 0.0 copy-done
  3.9 0.0 copy-done.1
  3.9 0.0 copy-done.4
  4.0 0.0 copy-done.3
  4.0 0.0 copy-done.2
  4.0 0.8 %shard_map.78 = (f32[416,128]{1,0:T(8,128)S(1)}, f32[416,128]{1,0:T(8,128)S(1)}) custom-call(s32[2]{0:T(128)S(1)} %copy-done.4, s32[2,128]{1,0:T(2,128)S(1)} %copy-done.1, s32[2,128]{1,0:T(2,128)S(1)} %copy-done.1, f32[2,128]{1,0:T(2,128)S(1)} %copy-done.2, f32[2,128]{1,0:T(2,128)S(1)} %copy-done.3, f32[32,128]{1,0:T(8,128)S(1)} %bitcast.3, ...), custom_call_target="tpu_custom_call" | custom-call | tf_op jit(solution)/shard_map/pallas_call | solution.py:372
  4.8 0.5 %collective-permute-start = (f32[416,128]{1,0:T(8,128)S(1)}, f32[416,128]{1,0:T(8,128)S(1)}, u32[]{:S(2)}, u32[]{:S(2)}) collective-permute-start(f32[416,128]{1,0:T(8,128)S(1)} %get-tuple-element.7), channel_id=1, source_target_pairs={{0,1},{1,0},{2,3},{3,2},{4,5},{5,4},{6,7},{7,6},{8,9},{9,8},{10,11... | collective-permute-start | bytes 638984 | tf_op jit(solution)/shard_map/ppermute | solution.py:407
  5.3 1.1 %collective-permute-done = f32[416,128]{1,0:T(8,128)S(1)} collective-permute-done((f32[416,128]{1,0:T(8,128)S(1)}, f32[416,128]{1,0:T(8,128)S(1)}, u32[]{:S(2)}, u32[]{:S(2)}) %collective-permute-start) | collective-permute-done | bytes 213024 | tf_op jit(solution)/shard_map/ppermute | solution.py:407
  6.5 3.0 %collective-permute-start.1 = (f32[208,128]{1,0:T(8,128)S(1)}, f32[208,128]{1,0:T(8,128)S(1)}, u32[]{:S(2)}, u32[]{:S(2)}) collective-permute-start(f32[208,128]{1,0:T(8,128)S(1)} %slice_select_fusion), channel_id=1, source_target_pairs={{0,2},{1,3},{2,0},{3,1},{4,6},{5,7},{6,4},{7,5},{8,10},{9,11},{10,... | collective-permute-start | bytes 319496 | tf_op jit(solution)/shard_map/ppermute | solution.py:407
  9.4 3.3 %collective-permute-done.1 = f32[208,128]{1,0:T(8,128)S(1)} collective-permute-done((f32[208,128]{1,0:T(8,128)S(1)}, f32[208,128]{1,0:T(8,128)S(1)}, u32[]{:S(2)}, u32[]{:S(2)}) %collective-permute-start.1) | collective-permute-done | bytes 106528 | tf_op jit(solution)/shard_map/ppermute | solution.py:407
  12.7 3.1 %collective-permute-start.2 = (f32[208,128]{1,0:T(8,128)S(1)}, f32[208,128]{1,0:T(8,128)S(1)}, u32[]{:S(2)}, u32[]{:S(2)}) collective-permute-start(f32[208,128]{1,0:T(8,128)S(1)} %select_add_fusion), channel_id=1, source_target_pairs={{0,4},{1,5},{2,6},{3,7},{4,0},{5,1},{6,2},{7,3},{8,12},{9,13},{10,... | collective-permute-start | bytes 319496 | tf_op jit(solution)/shard_map/ppermute | solution.py:407
  15.8 2.7 %collective-permute-done.2 = f32[208,128]{1,0:T(8,128)S(1)} collective-permute-done((f32[208,128]{1,0:T(8,128)S(1)}, f32[208,128]{1,0:T(8,128)S(1)}, u32[]{:S(2)}, u32[]{:S(2)}) %collective-permute-start.2) | collective-permute-done | bytes 106528 | tf_op jit(solution)/shard_map/ppermute | solution.py:407
  18.5 2.8 %collective-permute-start.3 = (f32[208,128]{1,0:T(8,128)S(1)}, f32[208,128]{1,0:T(8,128)S(1)}, u32[]{:S(2)}, u32[]{:S(2)}) collective-permute-start(f32[208,128]{1,0:T(8,128)S(1)} %add.14), channel_id=1, source_target_pairs={{0,8},{1,9},{2,10},{3,11},{4,12},{5,13},{6,14},{7,15},{8,0},{9,1},... | collective-permute-start | bytes 319496 | tf_op jit(solution)/shard_map/ppermute | solution.py:407
  21.3 4.5 %collective-permute-done.3 = f32[208,128]{1,0:T(8,128)S(1)} collective-permute-done((f32[208,128]{1,0:T(8,128)S(1)}, f32[208,128]{1,0:T(8,128)S(1)}, u32[]{:S(2)}, u32[]{:S(2)}) %collective-permute-start.3) | collective-permute-done | bytes 106528 | tf_op jit(solution)/shard_map/ppermute | solution.py:407
  25.8 0.1 collective-permute-start.4
  25.9 4.7 %collective-permute-done.4 = f32[208,128]{1,0:T(8,128)S(1)} collective-permute-done((f32[208,128]{1,0:T(8,128)S(1)}, f32[208,128]{1,0:T(8,128)S(1)}, u32[]{:S(2)}, u32[]{:S(2)}) %collective-permute-start.4) | collective-permute-done | bytes 106528 | tf_op jit(solution)/shard_map/ppermute | solution.py:407
  30.6 0.1 collective-permute-start.5
  30.7 1.5 %collective-permute-done.5.other_v = f32[416,128]{1,0:T(8,128)S(1)} collective-permute-done((f32[416,128]{1,0:T(8,128)S(1)}, f32[416,128]{1,0:T(8,128)S(1)}, u32[]{:S(2)}, u32[]{:S(2)}) %collective-permute-start.5) | collective-permute-done | bytes 213024 | tf_op jit(solution)/shard_map/ppermute | solution.py:407
  32.1 14.2 %shard_map.79 = (f32[4096,256]{1,0:T(8,128)}, f32[1,4096]{1,0:T(1,128)}) custom-call(f32[416,128]{1,0:T(8,128)S(1)} %pad_maximum_fusion.mine_v, f32[416,128]{1,0:T(8,128)S(1)} %collective-permute-done.5.other_v, f32[1,4096]{1,0:T(1,128)S(1)} %bitcast.4, f32[4096,256]{1,0:T(8,128)} %x_hbm.5), custom_call_target="tpu_custom_call" | custom-call | tf_op jit(solution)/shard_map/pallas_call | solution.py:389
  (7 shorter events, 0.1 us)
Async XLA Ops:
  0.6 3.3 %copy-start = (f32[4096]{0:T(1024)S(1)}, f32[4096]{0:T(1024)}, u32[]{:S(2)}) copy-start(f32[4096]{0:T(1024)} %param.7) | copy-start | bytes 49156
  0.6 3.3 %copy-start.1 = (s32[2,128]{1,0:T(2,128)S(1)}, s32[2,128]{1,0:T(2,128)}, u32[]{:S(2)}) copy-start(s32[2,128]{1,0:T(2,128)} %rows_v.1) | copy-start | bytes 3076
  0.7 3.3 %copy-start.4 = (s32[2]{0:T(128)S(1)}, s32[2]{0:T(128)}, u32[]{:S(2)}) copy-start(s32[2]{0:T(128)} %owner_s.1) | copy-start | bytes 28
  0.7 3.3 %copy-start.3 = (f32[2,128]{1,0:T(2,128)S(1)}, f32[2,128]{1,0:T(2,128)}, u32[]{:S(2)}) copy-start(f32[2,128]{1,0:T(2,128)} %error_var.1) | copy-start | bytes 3076
  0.7 3.3 %copy-start.2 = (f32[2,128]{1,0:T(2,128)S(1)}, f32[2,128]{1,0:T(2,128)}, u32[]{:S(2)}) copy-start(f32[2,128]{1,0:T(2,128)} %observed.1) | copy-start | bytes 3076
  4.8 1.6 %collective-permute-start = (f32[416,128]{1,0:T(8,128)S(1)}, f32[416,128]{1,0:T(8,128)S(1)}, u32[]{:S(2)}, u32[]{:S(2)}) collective-permute-start(f32[416,128]{1,0:T(8,128)S(1)} %get-tuple-element.7), channel_id=1, source_target_pairs={{0,1},{1,0},{2,3},{3,2},{4,5},{5,4},{6,7},{7,6},{8,9},{9,8},{10,11... | collective-permute-start | bytes 638984 | tf_op jit(solution)/shard_map/ppermute | solution.py:407
  6.5 6.2 %collective-permute-start.1 = (f32[208,128]{1,0:T(8,128)S(1)}, f32[208,128]{1,0:T(8,128)S(1)}, u32[]{:S(2)}, u32[]{:S(2)}) collective-permute-start(f32[208,128]{1,0:T(8,128)S(1)} %slice_select_fusion), channel_id=1, source_target_pairs={{0,2},{1,3},{2,0},{3,1},{4,6},{5,7},{6,4},{7,5},{8,10},{9,11},{10,... | collective-permute-start | bytes 319496 | tf_op jit(solution)/shard_map/ppermute | solution.py:407
  12.7 5.8 %collective-permute-start.2 = (f32[208,128]{1,0:T(8,128)S(1)}, f32[208,128]{1,0:T(8,128)S(1)}, u32[]{:S(2)}, u32[]{:S(2)}) collective-permute-start(f32[208,128]{1,0:T(8,128)S(1)} %select_add_fusion), channel_id=1, source_target_pairs={{0,4},{1,5},{2,6},{3,7},{4,0},{5,1},{6,2},{7,3},{8,12},{9,13},{10,... | collective-permute-start | bytes 319496 | tf_op jit(solution)/shard_map/ppermute | solution.py:407
  18.5 7.3 %collective-permute-start.3 = (f32[208,128]{1,0:T(8,128)S(1)}, f32[208,128]{1,0:T(8,128)S(1)}, u32[]{:S(2)}, u32[]{:S(2)}) collective-permute-start(f32[208,128]{1,0:T(8,128)S(1)} %add.14), channel_id=1, source_target_pairs={{0,8},{1,9},{2,10},{3,11},{4,12},{5,13},{6,14},{7,15},{8,0},{9,1},... | collective-permute-start | bytes 319496 | tf_op jit(solution)/shard_map/ppermute | solution.py:407
  25.8 4.8 %collective-permute-start.4 = (f32[208,128]{1,0:T(8,128)S(1)}, f32[208,128]{1,0:T(8,128)S(1)}, u32[]{:S(2)}, u32[]{:S(2)}) collective-permute-start(f32[208,128]{1,0:T(8,128)S(1)} %add.15), channel_id=1, source_target_pairs={{0,2},{1,3},{2,0},{3,1},{4,6},{5,7},{6,4},{7,5},{8,10},{9,11},{10,... | collective-permute-start | bytes 319496 | tf_op jit(solution)/shard_map/ppermute | solution.py:407
  30.6 1.5 %collective-permute-start.5 = (f32[416,128]{1,0:T(8,128)S(1)}, f32[416,128]{1,0:T(8,128)S(1)}, u32[]{:S(2)}, u32[]{:S(2)}) collective-permute-start(f32[416,128]{1,0:T(8,128)S(1)} %pad_maximum_fusion.mine_v), channel_id=1, source_target_pairs={{0,1},{1,0},{2,3},{3,2},{4,5},{5,4},{6,7},{7,6},{8,9},{9,8},{10,11... | collective-permute-start | bytes 638984 | tf_op jit(solution)/shard_map/ppermute | solution.py:407

commit v4 on v3

--- a/solution.py
+++ b/solution.py
@@ -53,8 +53,8 @@
 def gram_kernel(x_hbm, out, x_buf, sem):
     rows, members = x_buf.shape
     half = members // 2
-    quarter = rows // 4
-    pieces = [(0, quarter), (quarter, quarter), (2 * quarter, rows - 2 * quarter)]
+    cut = 3 * rows // 8
+    pieces = [(0, cut), (cut, rows - cut)]
     load, every_load = piece_copy(x_hbm, x_buf, sem, pieces)
     every_load(lambda copy: copy.start())
     total = None
@@ -360,7 +360,7 @@
         out_shape=jax.ShapeDtypeStruct((PACKED - G00, LANES), F32),
         in_specs=[spec(pltpu.HBM)],
         out_specs=spec(pltpu.VMEM),
-        scratch_shapes=[pltpu.VMEM((rows, members), F32), pltpu.SemaphoreType.DMA((3,))],
+        scratch_shapes=[pltpu.VMEM((rows, members), F32), pltpu.SemaphoreType.DMA((2,))],
         cost_estimate=cost(4 * rows * members * members, 4 * rows * members),
         compiler_params=params(),
     )(ensemble)

time: 46.5 us -> 47 us (1.011)
  starting transfers between devices: 9.51 us -> 8.4 us
  waiting for transfers between devices: 17.7 us -> 18.5 us
  Pallas kernels: 18.2 us -> 18.7 us
    ppermute x6, starting transfers between devices: 9.51 us -> 8.4 us  [swap(): return lax.ppermute(value, AXIS, [(i, i ^ mask) for i in range(count)])]
    ppermute x6, waiting for transfers between devices: 17.7 us -> 18.5 us  [swap(): return lax.ppermute(value, AXIS, [(i, i ^ mask) for i in range(count)])]
where the time goes in v4:
time: 47 us; the launch traced here: 46.7 us
  Pallas kernels  18.7 us (40%)
  waiting for transfers between devices  18.5 us (39%)
  starting transfers between devices  8.4 us (18%)
  between operations  0.93 us (2%)
    ppermute x6, waiting for transfers between devices, swap(): return lax.ppermute(value, AXIS, [(i, i ^ mask) for i in range(count)])  18.5 us
    pallas_call x1, Pallas kernels, update(): pl.pallas_call(functools.partial(update_kernel, chunks), out_shape=(jax.S...  14.2 us
    ppermute x6, starting transfers between devices, swap(): return lax.ppermute(value, AXIS, [(i, i ^ mask) for i in range(count)])  8.4 us
    pallas_call x1, Pallas kernels, gram_of(): pl.pallas_call(gram_kernel, out_shape=jax.ShapeDtypeStruct((PACKED - G00,...  3.69 us
  transfers between devices with their start and end apart: 6, of which 6 were waited for; matrix products, arithmetic and copies ran while one was open for 0% of the time, Pallas kernels for 0%

profile of v4, /device:TPU:0, one launch (start us, length us, event | category | flops | bytes accessed | tf_op | source)
XLA Modules:
  0.0 46.7 jit_solution(16257210460864795057)
XLA Ops:
  0.6 0.0 copy-start
  0.6 0.0 copy-start.1
  0.7 0.0 copy-start.4
  0.7 0.0 copy-start.3
  0.7 0.0 copy-start.2
  0.7 3.7 %shard_map.77.gram = f32[320,128]{1,0:T(8,128)S(1)} custom-call(f32[4096,256]{1,0:T(8,128)} %x_hbm.5), custom_call_target="tpu_custom_call" | custom-call | flops 1073741824 | bytes 4194304 | tf_op jit(solution)/shard_map/pallas_call | solution.py:358
  4.4 0.0 copy-done
  4.4 0.0 copy-done.1
  4.4 0.0 copy-done.4
  4.4 0.0 copy-done.3
  4.4 0.0 copy-done.2
  4.4 0.8 %shard_map.78 = (f32[416,128]{1,0:T(8,128)S(1)}, f32[416,128]{1,0:T(8,128)S(1)}) custom-call(s32[2]{0:T(128)S(1)} %copy-done.4, s32[2,128]{1,0:T(2,128)S(1)} %copy-done.1, s32[2,128]{1,0:T(2,128)S(1)} %copy-done.1, f32[2,128]{1,0:T(2,128)S(1)} %copy-done.2, f32[2,128]{1,0:T(2,128)S(1)} %copy-done.3, f32[32,128]{1,0:T(8,128)S(1)} %bitcast.3, ...), custom_call_target="tpu_custom_call" | custom-call | tf_op jit(solution)/shard_map/pallas_call | solution.py:372
  5.3 2.1 %collective-permute-start = (f32[416,128]{1,0:T(8,128)S(1)}, f32[416,128]{1,0:T(8,128)S(1)}, u32[]{:S(2)}, u32[]{:S(2)}) collective-permute-start(f32[416,128]{1,0:T(8,128)S(1)} %get-tuple-element.7), channel_id=1, source_target_pairs={{0,1},{1,0},{2,3},{3,2},{4,5},{5,4},{6,7},{7,6},{8,9},{9,8},{10,11... | collective-permute-start | bytes 638984 | tf_op jit(solution)/shard_map/ppermute | solution.py:407
  7.3 1.1 %collective-permute-done = f32[416,128]{1,0:T(8,128)S(1)} collective-permute-done((f32[416,128]{1,0:T(8,128)S(1)}, f32[416,128]{1,0:T(8,128)S(1)}, u32[]{:S(2)}, u32[]{:S(2)}) %collective-permute-start) | collective-permute-done | bytes 213024 | tf_op jit(solution)/shard_map/ppermute | solution.py:407
  8.5 2.4 %collective-permute-start.1 = (f32[208,128]{1,0:T(8,128)S(1)}, f32[208,128]{1,0:T(8,128)S(1)}, u32[]{:S(2)}, u32[]{:S(2)}) collective-permute-start(f32[208,128]{1,0:T(8,128)S(1)} %slice_select_fusion), channel_id=1, source_target_pairs={{0,2},{1,3},{2,0},{3,1},{4,6},{5,7},{6,4},{7,5},{8,10},{9,11},{10,... | collective-permute-start | bytes 319496 | tf_op jit(solution)/shard_map/ppermute | solution.py:407
  10.9 3.5 %collective-permute-done.1 = f32[208,128]{1,0:T(8,128)S(1)} collective-permute-done((f32[208,128]{1,0:T(8,128)S(1)}, f32[208,128]{1,0:T(8,128)S(1)}, u32[]{:S(2)}, u32[]{:S(2)}) %collective-permute-start.1) | collective-permute-done | bytes 106528 | tf_op jit(solution)/shard_map/ppermute | solution.py:407
  14.4 0.6 %collective-permute-start.2 = (f32[208,128]{1,0:T(8,128)S(1)}, f32[208,128]{1,0:T(8,128)S(1)}, u32[]{:S(2)}, u32[]{:S(2)}) collective-permute-start(f32[208,128]{1,0:T(8,128)S(1)} %select_add_fusion), channel_id=1, source_target_pairs={{0,4},{1,5},{2,6},{3,7},{4,0},{5,1},{6,2},{7,3},{8,12},{9,13},{10,... | collective-permute-start | bytes 319496 | tf_op jit(solution)/shard_map/ppermute | solution.py:407
  15.0 4.1 %collective-permute-done.2 = f32[208,128]{1,0:T(8,128)S(1)} collective-permute-done((f32[208,128]{1,0:T(8,128)S(1)}, f32[208,128]{1,0:T(8,128)S(1)}, u32[]{:S(2)}, u32[]{:S(2)}) %collective-permute-start.2) | collective-permute-done | bytes 106528 | tf_op jit(solution)/shard_map/ppermute | solution.py:407
  19.2 1.6 %collective-permute-start.3 = (f32[208,128]{1,0:T(8,128)S(1)}, f32[208,128]{1,0:T(8,128)S(1)}, u32[]{:S(2)}, u32[]{:S(2)}) collective-permute-start(f32[208,128]{1,0:T(8,128)S(1)} %add.14), channel_id=1, source_target_pairs={{0,8},{1,9},{2,10},{3,11},{4,12},{5,13},{6,14},{7,15},{8,0},{9,1},... | collective-permute-start | bytes 319496 | tf_op jit(solution)/shard_map/ppermute | solution.py:407
  20.8 5.2 %collective-permute-done.3 = f32[208,128]{1,0:T(8,128)S(1)} collective-permute-done((f32[208,128]{1,0:T(8,128)S(1)}, f32[208,128]{1,0:T(8,128)S(1)}, u32[]{:S(2)}, u32[]{:S(2)}) %collective-permute-start.3) | collective-permute-done | bytes 106528 | tf_op jit(solution)/shard_map/ppermute | solution.py:407
  26.0 1.6 %collective-permute-start.4 = (f32[208,128]{1,0:T(8,128)S(1)}, f32[208,128]{1,0:T(8,128)S(1)}, u32[]{:S(2)}, u32[]{:S(2)}) collective-permute-start(f32[208,128]{1,0:T(8,128)S(1)} %add.15), channel_id=1, source_target_pairs={{0,2},{1,3},{2,0},{3,1},{4,6},{5,7},{6,4},{7,5},{8,10},{9,11},{10,... | collective-permute-start | bytes 319496 | tf_op jit(solution)/shard_map/ppermute | solution.py:407
  27.6 3.2 %collective-permute-done.4 = f32[208,128]{1,0:T(8,128)S(1)} collective-permute-done((f32[208,128]{1,0:T(8,128)S(1)}, f32[208,128]{1,0:T(8,128)S(1)}, u32[]{:S(2)}, u32[]{:S(2)}) %collective-permute-start.4) | collective-permute-done | bytes 106528 | tf_op jit(solution)/shard_map/ppermute | solution.py:407
  30.8 0.1 collective-permute-start.5
  30.9 1.5 %collective-permute-done.5.other_v = f32[416,128]{1,0:T(8,128)S(1)} collective-permute-done((f32[416,128]{1,0:T(8,128)S(1)}, f32[416,128]{1,0:T(8,128)S(1)}, u32[]{:S(2)}, u32[]{:S(2)}) %collective-permute-start.5) | collective-permute-done | bytes 213024 | tf_op jit(solution)/shard_map/ppermute | solution.py:407
  32.4 14.2 %shard_map.79 = (f32[4096,256]{1,0:T(8,128)}, f32[1,4096]{1,0:T(1,128)}) custom-call(f32[416,128]{1,0:T(8,128)S(1)} %pad_maximum_fusion.mine_v, f32[416,128]{1,0:T(8,128)S(1)} %collective-permute-done.5.other_v, f32[1,4096]{1,0:T(1,128)S(1)} %bitcast.4, f32[4096,256]{1,0:T(8,128)} %x_hbm.5), custom_call_target="tpu_custom_call" | custom-call | tf_op jit(solution)/shard_map/pallas_call | solution.py:389
  (7 shorter events, 0.1 us)
Async XLA Ops:
  0.6 3.8 %copy-start = (f32[4096]{0:T(1024)S(1)}, f32[4096]{0:T(1024)}, u32[]{:S(2)}) copy-start(f32[4096]{0:T(1024)} %param.7) | copy-start | bytes 49156
  0.6 3.8 %copy-start.1 = (s32[2,128]{1,0:T(2,128)S(1)}, s32[2,128]{1,0:T(2,128)}, u32[]{:S(2)}) copy-start(s32[2,128]{1,0:T(2,128)} %rows_v.1) | copy-start | bytes 3076
  0.7 3.8 %copy-start.4 = (s32[2]{0:T(128)S(1)}, s32[2]{0:T(128)}, u32[]{:S(2)}) copy-start(s32[2]{0:T(128)} %owner_s.1) | copy-start | bytes 28
  0.7 3.8 %copy-start.3 = (f32[2,128]{1,0:T(2,128)S(1)}, f32[2,128]{1,0:T(2,128)}, u32[]{:S(2)}) copy-start(f32[2,128]{1,0:T(2,128)} %error_var.1) | copy-start | bytes 3076
  0.7 3.8 %copy-start.2 = (f32[2,128]{1,0:T(2,128)S(1)}, f32[2,128]{1,0:T(2,128)}, u32[]{:S(2)}) copy-start(f32[2,128]{1,0:T(2,128)} %observed.1) | copy-start | bytes 3076
  5.3 3.1 %collective-permute-start = (f32[416,128]{1,0:T(8,128)S(1)}, f32[416,128]{1,0:T(8,128)S(1)}, u32[]{:S(2)}, u32[]{:S(2)}) collective-permute-start(f32[416,128]{1,0:T(8,128)S(1)} %get-tuple-element.7), channel_id=1, source_target_pairs={{0,1},{1,0},{2,3},{3,2},{4,5},{5,4},{6,7},{7,6},{8,9},{9,8},{10,11... | collective-permute-start | bytes 638984 | tf_op jit(solution)/shard_map/ppermute | solution.py:407
  8.5 5.9 %collective-permute-start.1 = (f32[208,128]{1,0:T(8,128)S(1)}, f32[208,128]{1,0:T(8,128)S(1)}, u32[]{:S(2)}, u32[]{:S(2)}) collective-permute-start(f32[208,128]{1,0:T(8,128)S(1)} %slice_select_fusion), channel_id=1, source_target_pairs={{0,2},{1,3},{2,0},{3,1},{4,6},{5,7},{6,4},{7,5},{8,10},{9,11},{10,... | collective-permute-start | bytes 319496 | tf_op jit(solution)/shard_map/ppermute | solution.py:407
  14.4 4.8 %collective-permute-start.2 = (f32[208,128]{1,0:T(8,128)S(1)}, f32[208,128]{1,0:T(8,128)S(1)}, u32[]{:S(2)}, u32[]{:S(2)}) collective-permute-start(f32[208,128]{1,0:T(8,128)S(1)} %select_add_fusion), channel_id=1, source_target_pairs={{0,4},{1,5},{2,6},{3,7},{4,0},{5,1},{6,2},{7,3},{8,12},{9,13},{10,... | collective-permute-start | bytes 319496 | tf_op jit(solution)/shard_map/ppermute | solution.py:407
  19.2 6.8 %collective-permute-start.3 = (f32[208,128]{1,0:T(8,128)S(1)}, f32[208,128]{1,0:T(8,128)S(1)}, u32[]{:S(2)}, u32[]{:S(2)}) collective-permute-start(f32[208,128]{1,0:T(8,128)S(1)} %add.14), channel_id=1, source_target_pairs={{0,8},{1,9},{2,10},{3,11},{4,12},{5,13},{6,14},{7,15},{8,0},{9,1},... | collective-permute-start | bytes 319496 | tf_op jit(solution)/shard_map/ppermute | solution.py:407
  26.0 4.8 %collective-permute-start.4 = (f32[208,128]{1,0:T(8,128)S(1)}, f32[208,128]{1,0:T(8,128)S(1)}, u32[]{:S(2)}, u32[]{:S(2)}) collective-permute-start(f32[208,128]{1,0:T(8,128)S(1)} %add.15), channel_id=1, source_target_pairs={{0,2},{1,3},{2,0},{3,1},{4,6},{5,7},{6,4},{7,5},{8,10},{9,11},{10,... | collective-permute-start | bytes 319496 | tf_op jit(solution)/shard_map/ppermute | solution.py:407
  30.8 1.5 %collective-permute-start.5 = (f32[416,128]{1,0:T(8,128)S(1)}, f32[416,128]{1,0:T(8,128)S(1)}, u32[]{:S(2)}, u32[]{:S(2)}) collective-permute-start(f32[416,128]{1,0:T(8,128)S(1)} %pad_maximum_fusion.mine_v), channel_id=1, source_target_pairs={{0,1},{1,0},{2,3},{3,2},{4,5},{5,4},{6,7},{7,6},{8,9},{9,8},{10,11... | collective-permute-start | bytes 638984 | tf_op jit(solution)/shard_map/ppermute | solution.py:407
